TPU v7x, 32 devices: a whole 2x2x4 slice. The times are simulated.
32 devices in a mesh: row: 2 (over y), col: 4 (over z), depth: 4 (over x, core).
Axes of the slice: x: 2, y: 2, z: 4, core: 2. Of those that a mesh axis runs over, the one named last changes fastest.
Arguments:
- a_tiles: bfloat16 [2, 4, 4, 4, 128, 128], P('row', 'col', 'depth'), may hold values from -0.625 to 0.625
- pair_lists: int32 [2, 4, 4, 4, 2, 4, 12], P('row', 'col', 'depth'), may hold values from 0 to 7, as said below
Outputs:
- product_blocks: float32 [2, 4, 12, 128, 128], P('row', 'col', 'depth')
Inputs may be any that keep to these rules, and one draw needn't show every extreme that they name: pair_lists[..., 0, m, o] is a left slot below 4, or 4 for an empty pair slot; the live pairs of a product block come first; pair_lists[..., 1, m, o] is a slot of the right panel.
All inputs are finite; a program needn't handle non-finite values.
Results may differ from a plain program's by a relative error of at most 0.0003.
Values may be sent and summed in bfloat16 or wider, within the bound.
No kernel may reach another device: no remote copies, remote signals or barrier semaphores. Data moves between devices by JAX's collectives and lax.ppermute only.
A program may use at most 64 MiB of HBM per device.

v0:
```python
import jax
import jax.numpy as jnp
from jax import lax
from jax.sharding import PartitionSpec as P


def from_behind(block, axis, distance):
    devices = range(lax.axis_size(axis))
    route = [((i - distance) % len(devices), i) for i in devices]
    return lax.ppermute(block, axis, route)


def body(a_tiles, pair_lists):
    slot_count = a_tiles.shape[3]
    block_width = a_tiles.shape[4]
    own_tiles = a_tiles.reshape(slot_count, block_width, block_width)
    pair_table = pair_lists.reshape(pair_lists.shape[3:])
    shift_count = pair_table.shape[0]
    right_panel = lax.all_gather(own_tiles, "row", axis=0, tiled=True)
    zero_block = jnp.zeros((1, block_width, block_width), jnp.bfloat16)

    def contract(left_set, left_index, right_index):
        chosen = jnp.take(left_set, left_index, axis=0)
        partner = jnp.take(right_panel, right_index, axis=0)
        return jnp.einsum("moik,mojk->oij", chosen, partner, preferred_element_type=jnp.float32)

    def advance(step_index, carried):
        panel_tile, running = carried
        shifted = from_behind(panel_tile, "col", 1)
        padded = jnp.concatenate([shifted, zero_block], axis=0)
        return (
            shifted,
            running + contract(padded, pair_table[step_index, 0], pair_table[step_index, 1]),
        )

    opening = contract(
        jnp.concatenate([own_tiles, zero_block], axis=0), pair_table[0, 0], pair_table[0, 1]
    )
    carried = lax.fori_loop(1, shift_count, advance, (own_tiles, opening))
    running = carried[1]
    reduced = lax.psum_scatter(running, "depth", scatter_dimension=0, tiled=True)
    return reduced.reshape((1, 1) + reduced.shape)


def solution(mesh):
    placed = (
        P("row", "col", "depth", None, None, None),
        P("row", "col", "depth", None, None, None, None),
    )
    return jax.shard_map(
        body,
        mesh=mesh,
        in_specs=placed,
        out_specs=P("row", "col", "depth", None, None),
        check_vma=False,
    )
```

profile of v0, /device:TPU:0, one launch (start us, length us, event | category | flops | bytes accessed | tf_op | source)
XLA Modules:
  0.0 84.0 jit_solution(15283094002733839597)
XLA Ops:
  6.5 0.9 %copy.60 = bf16[1,1,1,4,128,128]{5,4,3,2,1,0:T(8,128)(2,1)S(1)} copy(bf16[1,1,1,4,128,128]{5,4,3,2,1,0:T(8,128)(2,1)} %param.8) | data formatting | bytes 262144
  9.3 7.1 %all-gather = bf16[1,1,1,8,128,128]{5,4,2,1,0,3:T(8,128)(2,1)S(1)} all-gather(bf16[1,1,1,4,128,128]{5,4,2,1,0,3:T(8,128)(2,1)S(1)} %bitcast.47), channel_id=2, replica_groups=mesh['row'=2,'col'=4,'depth'=4] {'row'}, dimensions={3}, use_global_device_ids=true | all-gather | bytes 393216 | tf_op jit(solution)/shard_map/all_gather | solution.py:19
  16.4 0.8 %gather_fusion.2 = bf16[48,128,128]{2,1,0:T(8,128)(2,1)S(1)} fusion(bf16[5,128,128]{2,1,0:T(8,128)(2,1)S(1)} %concatenate.8, s32[1024]{0:T(1024)S(1)} %pad_clamp_fusion.3), kind=kCustom, calls=%fused_computation.2.clone | custom fusion | bytes 3145920 | tf_op jit(solution)/shard_map/jit(_take)/gather | solution.py:23
  17.2 0.8 %gather_fusion.3 = bf16[48,128,128]{2,1,0:T(8,128)(2,1)S(1)} fusion(bf16[8,128,128]{2,1,0:T(8,128)(2,1)S(1)} %bitcast.41, s32[1024]{0:T(1024)S(1)} %pad_clamp_fusion.2), kind=kCustom, calls=%fused_computation.3.clone | custom fusion | bytes 3145920 | tf_op jit(solution)/shard_map/jit(_take)/gather | solution.py:24
  18.1 1.6 %fusion.10 = f32[12,128,128]{2,1,0:T(8,128)} fusion(bf16[4,12,128,128]{3,2,1,0:T(8,128)(2,1)S(1)} %bitcast.46, pred[4,12]{0,1:T(8,128)(4,1)S(1)} %copy.17, bf16[4,12,128,128]{3,2,1,0:T(8,128)(2,1)S(1)} %bitcast.45, pred[4,12]{0,1:T(8,128)(4,1)S(1)} %copy.15), kind=kOutput, calls=%fused_computation.24 | convolution fusion | flops 202899456 | bytes 3932256 | tf_op jit(solution)/shard_map/moik,mojk->oij/dot_general | solution.py:25
  19.7 35.6 %while.17 = (s32[]{:T(128)}, bf16[4,128,128]{2,1,0:T(8,128)(2,1)S(1)}, f32[12,128,128]{2,1,0:T(8,128)}, s32[4,2,4,12]{3,2,1,0:T(4,128)}, bf16[8,128,128]{2,1,0:T...) while((s32[]{:T(128)}, bf16[4,128,128]{2,1,0:T(8,128)(2,1)S(1)}, ...), condition=%wide.region_1.0_spmd, body=%wide.region_0.3_spmd.sunk | while | flops 203098688 | bytes 18393956 | solution.py:39
  19.7 1.8 %collective-permute-start = (bf16[4,128,128]{2,1,0:T(8,128)(2,1)S(1)}, bf16[4,128,128]{2,1,0:T(8,128)(2,1)S(1)}, u32[]{:S(2)}, u32[]{:S(2)}) collective-permute-start(bf16[4,128,128]{2,1,0:T(8,128)(2,1)S(1)} %get-tuple-element.209), channel_id=1, source_target_pairs={{12,0},{0,4},{4,8},{8,12},{13,1},{1,5},{5,9},{9,13},{14,2},{2,6},{... | collective-permute-start | bytes 393224 | tf_op jit(solution)/shard_map/while/body/eval_jaxpr/ppermute | solution.py:10
  22.6 0.9 %gather_fusion = bf16[48,128,128]{2,1,0:T(8,128)(2,1)S(1)} fusion(bf16[8,128,128]{2,1,0:T(8,128)(2,1)S(1)} %get-tuple-element.221, s32[1024]{0:T(1024)S(1)} %pad_clamp_fusion.6), kind=kCustom, calls=%fused_computation.1.clone.clone.1 | custom fusion | bytes 3145920 | tf_op jit(solution)/shard_map/while/body/eval_jaxpr/jit(_take)/gather | solution.py:24
  23.5 3.0 %collective-permute-done = bf16[4,128,128]{2,1,0:T(8,128)(2,1)S(1)} collective-permute-done((bf16[4,128,128]{2,1,0:T(8,128)(2,1)S(1)}, bf16[4,128,128]{2,1,0:T(8,128)(2,1)S(1)}, u32[]{:S(2)}, u32[]{:S(2)}) %collective-permute-start) | collective-permute-done | bytes 131104 | tf_op jit(solution)/shard_map/while/body/eval_jaxpr/ppermute | solution.py:10
  26.5 1.9 %gather_fusion.1 = bf16[48,128,128]{2,1,0:T(8,128)(2,1)} fusion(bf16[5,128,128]{2,1,0:T(8,128)(2,1)S(1)} %concatenate.10, s32[1024]{0:T(1024)S(1)} %pad_clamp_fusion.7), kind=kCustom, calls=%fused_computation.clone.clone.1 | custom fusion | bytes 3145920 | tf_op jit(solution)/shard_map/while/body/eval_jaxpr/jit(_take)/gather | solution.py:23
  28.4 2.2 %fusion.14 = f32[12,128,128]{2,1,0:T(8,128)S(1)} fusion(f32[12,128,128]{2,1,0:T(8,128)S(1)} %copy-done, bf16[4,12,128,128]{3,2,1,0:T(8,128)(2,1)S(1)} %bitcast.43, pred[4,12]{0,1:T(8,128)(4,1)S(1)} %copy.48, bf16[4,12,128,128]{3,2,1,0:T(8,128)(2,1)} %bitcast.44, pred[4,12]{0,1:T(8,128)(4,1)S(1)} %copy.49), kind=kOutput, calls=%fused_computation.10.clone.1 | convolution fusion | flops 203096064 | bytes 4718688 | tf_op jit(solution)/shard_map/while/body/eval_jaxpr/moik,mojk->oij/dot_general | solution.py:25
  30.7 0.9 %copy-done.1 = f32[12,128,128]{2,1,0:T(8,128)} copy-done((f32[12,128,128]{2,1,0:T(8,128)}, f32[12,128,128]{2,1,0:T(8,128)S(1)}, u32[]{:S(2)}) %copy-start.1) | copy-done | bytes 786456 | tf_op jit(solution)/shard_map/while
  32.6 0.9 %gather_fusion = bf16[48,128,128]{2,1,0:T(8,128)(2,1)S(1)} fusion(bf16[8,128,128]{2,1,0:T(8,128)(2,1)S(1)} %get-tuple-element.221, s32[1024]{0:T(1024)S(1)} %pad_clamp_fusion.6), kind=kCustom, calls=%fused_computation.1.clone.clone.1 | custom fusion | bytes 3145920 | tf_op jit(solution)/shard_map/while/body/eval_jaxpr/jit(_take)/gather | solution.py:24
  33.5 4.8 %collective-permute-done = bf16[4,128,128]{2,1,0:T(8,128)(2,1)S(1)} collective-permute-done((bf16[4,128,128]{2,1,0:T(8,128)(2,1)S(1)}, bf16[4,128,128]{2,1,0:T(8,128)(2,1)S(1)}, u32[]{:S(2)}, u32[]{:S(2)}) %collective-permute-start) | collective-permute-done | bytes 131104 | tf_op jit(solution)/shard_map/while/body/eval_jaxpr/ppermute | solution.py:10
  38.3 1.9 %gather_fusion.1 = bf16[48,128,128]{2,1,0:T(8,128)(2,1)} fusion(bf16[5,128,128]{2,1,0:T(8,128)(2,1)S(1)} %concatenate.10, s32[1024]{0:T(1024)S(1)} %pad_clamp_fusion.7), kind=kCustom, calls=%fused_computation.clone.clone.1 | custom fusion | bytes 3145920 | tf_op jit(solution)/shard_map/while/body/eval_jaxpr/jit(_take)/gather | solution.py:23
  40.3 2.2 %fusion.14 = f32[12,128,128]{2,1,0:T(8,128)S(1)} fusion(f32[12,128,128]{2,1,0:T(8,128)S(1)} %copy-done, bf16[4,12,128,128]{3,2,1,0:T(8,128)(2,1)S(1)} %bitcast.43, pred[4,12]{0,1:T(8,128)(4,1)S(1)} %copy.48, bf16[4,12,128,128]{3,2,1,0:T(8,128)(2,1)} %bitcast.44, pred[4,12]{0,1:T(8,128)(4,1)S(1)} %copy.49), kind=kOutput, calls=%fused_computation.10.clone.1 | convolution fusion | flops 203096064 | bytes 4718688 | tf_op jit(solution)/shard_map/while/body/eval_jaxpr/moik,mojk->oij/dot_general | solution.py:25
  42.5 0.9 %copy-done.1 = f32[12,128,128]{2,1,0:T(8,128)} copy-done((f32[12,128,128]{2,1,0:T(8,128)}, f32[12,128,128]{2,1,0:T(8,128)S(1)}, u32[]{:S(2)}) %copy-start.1) | copy-done | bytes 786456 | tf_op jit(solution)/shard_map/while
  43.4 0.7 compare_and_fusion.5
  44.5 0.9 %gather_fusion = bf16[48,128,128]{2,1,0:T(8,128)(2,1)S(1)} fusion(bf16[8,128,128]{2,1,0:T(8,128)(2,1)S(1)} %get-tuple-element.221, s32[1024]{0:T(1024)S(1)} %pad_clamp_fusion.6), kind=kCustom, calls=%fused_computation.1.clone.clone.1 | custom fusion | bytes 3145920 | tf_op jit(solution)/shard_map/while/body/eval_jaxpr/jit(_take)/gather | solution.py:24
  45.4 4.8 %collective-permute-done = bf16[4,128,128]{2,1,0:T(8,128)(2,1)S(1)} collective-permute-done((bf16[4,128,128]{2,1,0:T(8,128)(2,1)S(1)}, bf16[4,128,128]{2,1,0:T(8,128)(2,1)S(1)}, u32[]{:S(2)}, u32[]{:S(2)}) %collective-permute-start) | collective-permute-done | bytes 131104 | tf_op jit(solution)/shard_map/while/body/eval_jaxpr/ppermute | solution.py:10
  50.2 1.9 %gather_fusion.1 = bf16[48,128,128]{2,1,0:T(8,128)(2,1)} fusion(bf16[5,128,128]{2,1,0:T(8,128)(2,1)S(1)} %concatenate.10, s32[1024]{0:T(1024)S(1)} %pad_clamp_fusion.7), kind=kCustom, calls=%fused_computation.clone.clone.1 | custom fusion | bytes 3145920 | tf_op jit(solution)/shard_map/while/body/eval_jaxpr/jit(_take)/gather | solution.py:23
  52.1 2.2 %fusion.14 = f32[12,128,128]{2,1,0:T(8,128)S(1)} fusion(f32[12,128,128]{2,1,0:T(8,128)S(1)} %copy-done, bf16[4,12,128,128]{3,2,1,0:T(8,128)(2,1)S(1)} %bitcast.43, pred[4,12]{0,1:T(8,128)(4,1)S(1)} %copy.48, bf16[4,12,128,128]{3,2,1,0:T(8,128)(2,1)} %bitcast.44, pred[4,12]{0,1:T(8,128)(4,1)S(1)} %copy.49), kind=kOutput, calls=%fused_computation.10.clone.1 | convolution fusion | flops 203096064 | bytes 4718688 | tf_op jit(solution)/shard_map/while/body/eval_jaxpr/moik,mojk->oij/dot_general | solution.py:25
  54.4 0.9 %copy-done.1 = f32[12,128,128]{2,1,0:T(8,128)} copy-done((f32[12,128,128]{2,1,0:T(8,128)}, f32[12,128,128]{2,1,0:T(8,128)S(1)}, u32[]{:S(2)}) %copy-start.1) | copy-done | bytes 786456 | tf_op jit(solution)/shard_map/while
  55.3 21.9 %reduce-scatter.2.cloned.1.call-done = f32[3,128,128]{2,1,0:T(8,128)} async-done(((f32[12,128,128]{2,1,0:T(8,128)}), f32[3,128,128]{2,1,0:T(8,128)}) %reduce-scatter.2.cloned.1.call-update) | async-done | bytes 196624 | tf_op jit(solution)/shard_map/reduce_scatter | solution.py:41
  (48 shorter events, 4.5 us)
Async XLA Ops:
  6.5 70.6 %reduce-scatter.2.cloned.1.call-start = ((), (), s32[]{:S(2)}) async-start(), calls=%async_computation.1 | async-start | bytes 983040 | tf_op jit(solution)/shard_map/reduce_scatter | solution.py:41
  19.7 6.8 %collective-permute-start = (bf16[4,128,128]{2,1,0:T(8,128)(2,1)S(1)}, bf16[4,128,128]{2,1,0:T(8,128)(2,1)S(1)}, u32[]{:S(2)}, u32[]{:S(2)}) collective-permute-start(bf16[4,128,128]{2,1,0:T(8,128)(2,1)S(1)} %get-tuple-element.209), channel_id=1, source_target_pairs={{12,0},{0,4},{4,8},{8,12},{13,1},{1,5},{5,9},{9,13},{14,2},{2,6},{... | collective-permute-start | bytes 393224 | tf_op jit(solution)/shard_map/while/body/eval_jaxpr/ppermute | solution.py:10
  26.5 2.0 %copy-start = (f32[12,128,128]{2,1,0:T(8,128)S(1)}, f32[12,128,128]{2,1,0:T(8,128)}, u32[]{:S(2)}) copy-start(f32[12,128,128]{2,1,0:T(8,128)} %get-tuple-element.210) | copy-start | bytes 2359300 | tf_op jit(solution)/shard_map/while
  30.6 0.9 %copy-start.1 = (f32[12,128,128]{2,1,0:T(8,128)}, f32[12,128,128]{2,1,0:T(8,128)S(1)}, u32[]{:S(2)}) copy-start(f32[12,128,128]{2,1,0:T(8,128)S(1)} %fusion.14) | copy-start | bytes 2359300 | tf_op jit(solution)/shard_map/while
  31.5 6.8 %collective-permute-start = (bf16[4,128,128]{2,1,0:T(8,128)(2,1)S(1)}, bf16[4,128,128]{2,1,0:T(8,128)(2,1)S(1)}, u32[]{:S(2)}, u32[]{:S(2)}) collective-permute-start(bf16[4,128,128]{2,1,0:T(8,128)(2,1)S(1)} %get-tuple-element.209), channel_id=1, source_target_pairs={{12,0},{0,4},{4,8},{8,12},{13,1},{1,5},{5,9},{9,13},{14,2},{2,6},{... | collective-permute-start | bytes 393224 | tf_op jit(solution)/shard_map/while/body/eval_jaxpr/ppermute | solution.py:10
  38.3 2.0 %copy-start = (f32[12,128,128]{2,1,0:T(8,128)S(1)}, f32[12,128,128]{2,1,0:T(8,128)}, u32[]{:S(2)}) copy-start(f32[12,128,128]{2,1,0:T(8,128)} %get-tuple-element.210) | copy-start | bytes 2359300 | tf_op jit(solution)/shard_map/while
  42.5 0.9 %copy-start.1 = (f32[12,128,128]{2,1,0:T(8,128)}, f32[12,128,128]{2,1,0:T(8,128)S(1)}, u32[]{:S(2)}) copy-start(f32[12,128,128]{2,1,0:T(8,128)S(1)} %fusion.14) | copy-start | bytes 2359300 | tf_op jit(solution)/shard_map/while
  43.4 6.8 %collective-permute-start = (bf16[4,128,128]{2,1,0:T(8,128)(2,1)S(1)}, bf16[4,128,128]{2,1,0:T(8,128)(2,1)S(1)}, u32[]{:S(2)}, u32[]{:S(2)}) collective-permute-start(bf16[4,128,128]{2,1,0:T(8,128)(2,1)S(1)} %get-tuple-element.209), channel_id=1, source_target_pairs={{12,0},{0,4},{4,8},{8,12},{13,1},{1,5},{5,9},{9,13},{14,2},{2,6},{... | collective-permute-start | bytes 393224 | tf_op jit(solution)/shard_map/while/body/eval_jaxpr/ppermute | solution.py:10
  50.2 2.0 %copy-start = (f32[12,128,128]{2,1,0:T(8,128)S(1)}, f32[12,128,128]{2,1,0:T(8,128)}, u32[]{:S(2)}) copy-start(f32[12,128,128]{2,1,0:T(8,128)} %get-tuple-element.210) | copy-start | bytes 2359300 | tf_op jit(solution)/shard_map/while
  54.3 0.9 %copy-start.1 = (f32[12,128,128]{2,1,0:T(8,128)}, f32[12,128,128]{2,1,0:T(8,128)S(1)}, u32[]{:S(2)}) copy-start(f32[12,128,128]{2,1,0:T(8,128)S(1)} %fusion.14) | copy-start | bytes 2359300 | tf_op jit(solution)/shard_map/while
Sparse Core Ops, SparseCore 0:
  55.4 21.6 reduce-scatter.1
where the time goes:
time: 84.3 us; the launch traced here: 84 us
  waiting for transfers between devices  34.4 us (41%)
  local copies, waits for them, and re-layouts  15.2 us (18%)
  between operations  13.4 us (16%)
  matrix products  8.18 us (10%)
  blocking collectives  7.12 us (8%)
  other arithmetic  3.57 us (4%)
  starting transfers between devices  1.84 us (2%)
    reduce_scatter x1, waiting for transfers between devices, body(): lax.psum_scatter(running, 'depth', scatter_dimension=0, tiled=True)  21.9 us
    ppermute x3, waiting for transfers between devices, from_behind(): return lax.ppermute(block, axis, route)  12.6 us
    dot_general x4, matrix products, contract(): jnp.einsum('moik,mojk->oij', chosen, partner, preferred_element_type=jnp....  8.18 us
    all_gather x1, blocking collectives, body(): right_panel = lax.all_gather(own_tiles, 'row', axis=0, tiled=True)  7.12 us
    gather x4, local copies, waits for them, and re-layouts, contract(): chosen = jnp.take(left_set, left_index, axis=0)  6.69 us
    gather x4, local copies, waits for them, and re-layouts, contract(): partner = jnp.take(right_panel, right_index, axis=0)  3.4 us
    and x4, other arithmetic, contract(): chosen = jnp.take(left_set, left_index, axis=0)  2.82 us
    while x15, local copies, waits for them, and re-layouts  2.63 us
  transfers between devices with their start and end apart: 4, of which 4 were waited for; matrix products, arithmetic and copies ran while one was open for 7% of the time, Pallas kernels for 0%

commit v1 on v0

v1 whole, which is shorter than its diff:
```python
import functools

import jax
import jax.numpy as jnp
from jax import lax
from jax.experimental import pallas as pl
from jax.experimental.pallas import tpu as pltpu
from jax.sharding import PartitionSpec as P

VMEM = pl.BlockSpec(memory_space=pltpu.VMEM)
SMEM = pl.BlockSpec(memory_space=pltpu.SMEM)


def exchange(block, axis, distance):
    size = lax.axis_size(axis)
    return lax.ppermute(block, axis, [(i, i ^ distance) for i in range(size)])


def bits_down(size):
    return [1 << b for b in reversed(range(size.bit_length() - 1))]


def table_kernel(sizes, lists, table):
    cols, depths, slots, pairs, outs = sizes
    row, col, layer = (lax.axis_index(name) for name in ("row", "col", "depth"))
    share = outs // depths
    zero_slot = lax.axis_size("row") * slots

    def at(step, carry):
        hop, group = step // depths, step % depths
        shift = lax.rem(col - (col ^ hop) + cols, cols)
        for i in range(share):
            out = (layer ^ group) * share + i
            for m in range(pairs):
                left = lists[0, 0, 0, shift, 0, m, out]
                right = lists[0, 0, 0, shift, 1, m, out]
                live = left < slots
                place = (row ^ (right // slots)) * slots + lax.rem(right, slots)
                base = ((hop * outs + group * share + i) * pairs + m) * 2
                table[base] = jnp.where(live, left, 0)
                table[base + 1] = jnp.where(live, place, zero_slot)
        return carry

    lax.fori_loop(0, cols * depths, at, 0)


def products(table, hop, out, outs, pairs, left, panel):
    total = None
    base = (hop * outs + out) * pairs * 2
    width = 2 if pairs % 2 == 0 else 1
    for m in range(0, pairs, width):
        lefts = [left[table[base + 2 * (m + j)]] for j in range(width)]
        rights = [panel[table[base + 2 * (m + j) + 1]] for j in range(width)]
        term = lax.dot_general(
            jnp.concatenate(lefts, 1),
            jnp.concatenate(rights, 1),
            (((1,), (1,)), ((), ())),
            preferred_element_type=jnp.float32,
        )
        total = term if total is None else total + term
    return total


def panel_kernel(rows, table, *refs):
    sources, panel = refs[:rows], refs[rows]
    slots = sources[0].shape[0]
    for i, source in enumerate(sources):
        panel[pl.ds(i * slots, slots)] = source[...]
    panel[rows * slots] = jnp.zeros(panel.shape[1:], panel.dtype)


def add_kernel(hops, pairs, started, sent_groups, kept_groups, share, table, panel, *refs):
    lefts, refs = refs[: len(hops)], refs[len(hops) :]
    if started:
        (sent_in, kept_in), refs = refs[:2], refs[2:]
    sent, kept = refs
    outs = (len(sent_groups) + len(kept_groups)) * share
    for groups, target, source in (
        (sent_groups, sent, sent_in if started else None),
        (kept_groups, kept, kept_in if started else None),
    ):
        for place, group in enumerate(groups):
            for i in range(share):
                total = source[place * share + i] if started else None
                for hop, left in zip(hops, lefts):
                    term = products(table, hop, group * share + i, outs, pairs, left, panel)
                    total = term if total is None else total + term
                target[place * share + i] = total


def in_vmem(x):
    return pltpu.with_memory_space_constraint(x, pltpu.VMEM)


def body(a_tiles, pair_lists):
    rows, cols, depths = (lax.axis_size(name) for name in ("row", "col", "depth"))
    slots, width = a_tiles.shape[3], a_tiles.shape[4]
    pairs, outs = pair_lists.shape[5:]
    share = outs // depths
    own = a_tiles.reshape(slots, width, width)

    lefts = {0: own}
    for bit in bits_down(cols):
        lefts.update({hop ^ bit: exchange(block, "col", bit) for hop, block in list(lefts.items())})
    rights = {0: own}
    for bit in bits_down(rows):
        rights.update({hop ^ bit: exchange(block, "row", bit) for hop, block in list(rights.items())})

    table = pl.pallas_call(
        functools.partial(table_kernel, (cols, depths, slots, pairs, outs)),
        out_shape=pltpu.SMEM((cols * outs * pairs * 2,), jnp.int32),
        in_specs=[SMEM],
        out_specs=SMEM,
        name="pair_table",
    )(pair_lists)
    table = pltpu.with_memory_space_constraint(table, pltpu.SMEM)
    panel = pl.pallas_call(
        functools.partial(panel_kernel, rows),
        out_shape=pltpu.VMEM((rows * slots + 1, width, width), a_tiles.dtype),
        in_specs=[SMEM] + [VMEM] * rows,
        out_specs=VMEM,
        name="right_panel",
    )(table, *[in_vmem(rights[i]) for i in range(rows)])

    sent_groups = [g for g in range(depths) if g & 1]
    kept_groups = [g for g in range(depths) if not g & 1]
    half = pltpu.VMEM((len(sent_groups) * share, width, width), jnp.float32)

    def add(hops, sums, name):
        block_flops = 2 * width**3 * pairs * outs
        return pl.pallas_call(
            functools.partial(
                add_kernel, hops, pairs, bool(sums), sent_groups, kept_groups, share
            ),
            out_shape=(half, half),
            in_specs=[SMEM] + [VMEM] * (1 + len(hops) + len(sums)),
            out_specs=(VMEM, VMEM),
            name=name,
            cost_estimate=pl.CostEstimate(
                flops=block_flops * len(hops), bytes_accessed=0, transcendentals=0
            ),
        )(table, in_vmem(panel), *[in_vmem(lefts[h]) for h in hops], *[in_vmem(s) for s in sums])

    last = cols - 1
    sums = add(list(range(last)), (), "early_products")
    sent, kept = add([last], sums, "late_products")

    kept = kept.reshape(len(kept_groups), share, width, width)
    kept = kept + exchange(sent, "depth", 1).reshape(kept.shape)
    bit = 2
    while bit < depths:
        kept = kept.reshape(kept.shape[0] // 2, 2, share, width, width)
        kept = kept[:, 0] + exchange(kept[:, 1], "depth", bit)
        bit *= 2
    return kept.reshape(1, 1, share, width, width)


def solution(mesh):
    placed = (
        P("row", "col", "depth", None, None, None),
        P("row", "col", "depth", None, None, None, None),
    )
    return jax.shard_map(
        body,
        mesh=mesh,
        in_specs=placed,
        out_specs=P("row", "col", "depth", None, None),
        check_vma=False,
    )
```

time: 84.3 us -> 27.2 us (0.32)
  waiting for transfers between devices: 34.4 us -> 10.7 us
  local copies, waits for them, and re-layouts: 15.2 us -> 0.91 us
  between operations: 13.4 us -> 0.08 us
  matrix products: 8.18 us -> 0 us
  starting transfers between devices: 1.84 us -> 9.53 us
  blocking collectives: 7.12 us -> 0 us
  Pallas kernels: 0 us -> 5.02 us
  other arithmetic: 3.57 us -> 0.76 us
    reduce_scatter x1 -> x0, waiting for transfers between devices: 21.9 us -> none  [body(): lax.psum_scatter(running, 'depth', scatter_dimension=0, tiled=True)]
    gather x8 -> x0, local copies, waits for them, and re-layouts: 10.1 us -> none  [the longest x4 6.69 us: contract(): chosen = jnp.take(left_set, left_index, axis=0)]
    dot_general x4 -> x0, matrix products: 8.18 us -> none  [contract(): jnp.einsum('moik,mojk->oij', chosen, partner, preferred_element_type=jnp....]
    ppermute x3 -> x6, starting transfers between devices: 1.83 us -> 9.53 us  [exchange(): return lax.ppermute(block, axis, [(i, i ^ distance) for i in range(size)])]
    all_gather x1 -> x0, blocking collectives: 7.12 us -> none  [body(): right_panel = lax.all_gather(own_tiles, 'row', axis=0, tiled=True)]
    pallas_call x0 -> x4, Pallas kernels: none -> 5.02 us  [the longest x1 3.03 us: body(): pl.pallas_call(functools.partial(table_kernel, (cols, depths, slots, pair...]
    and x4 -> x0, other arithmetic: 2.82 us -> none  [contract(): chosen = jnp.take(left_set, left_index, axis=0)]
    while x15 -> x0, local copies, waits for them, and re-layouts: 2.63 us -> none
  transfers between devices with their start and end apart: 4 -> 6, of which waited for: 4 -> 3; matrix products, arithmetic and copies ran while one was open for 7% -> 0% of each run, Pallas kernels for 0% -> 16%
where the time goes in v1:
time: 27.2 us; the launch traced here: 27 us
  waiting for transfers between devices  10.7 us (39%)
  starting transfers between devices  9.53 us (35%)
  Pallas kernels  5.02 us (18%)
  local copies, waits for them, and re-layouts  0.91 us (3%)
  other arithmetic  0.76 us (3%)
    ppermute x6, waiting for transfers between devices, exchange(): return lax.ppermute(block, axis, [(i, i ^ distance) for i in range(size)])  10.7 us
    ppermute x6, starting transfers between devices, exchange(): return lax.ppermute(block, axis, [(i, i ^ distance) for i in range(size)])  9.53 us
    pallas_call x1, Pallas kernels, body(): pl.pallas_call(functools.partial(table_kernel, (cols, depths, slots, pair...  3.03 us
    pallas_call x2, Pallas kernels, add(): pl.pallas_call(functools.partial(add_kernel, hops, pairs, bool(sums), sen...  1.97 us
    unnamed x2, local copies, waits for them, and re-layouts  0.9 us
    reshape x1, other arithmetic, body(): return kept.reshape(1, 1, share, width, width)  0.7 us
  transfers between devices with their start and end apart: 6, of which 3 were waited for; matrix products, arithmetic and copies ran while one was open for 0% of the time, Pallas kernels for 16%

profile of v1, /device:TPU:0, one launch (start us, length us, event | category | flops | bytes accessed | tf_op | source)
XLA Modules:
  0.0 27.0 jit_solution(4318942091141523530)
XLA Ops:
  0.0 4.0 %collective-permute-start.1 = (bf16[4,128,128]{2,1,0:T(8,128)(2,1)}, bf16[4,128,128]{2,1,0:T(8,128)(2,1)S(1)}, u32[]{:S(2)}, u32[]{:S(2)}) collective-permute-start(bf16[4,128,128]{2,1,0:T(8,128)(2,1)} %bitcast.12), channel_id=1, source_target_pairs={{0,8},{4,12},{8,0},{12,4},{1,9},{5,13},{9,1},{13,5},{2,10},{6,14},... | collective-permute-start | bytes 393224 | tf_op jit(solution)/shard_map/ppermute | solution.py:16
  4.0 1.5 %collective-permute-start = (bf16[4,128,128]{2,1,0:T(8,128)(2,1)}, bf16[4,128,128]{2,1,0:T(8,128)(2,1)S(1)}, u32[]{:S(2)}, u32[]{:S(2)}) collective-permute-start(bf16[4,128,128]{2,1,0:T(8,128)(2,1)} %bitcast.13), channel_id=1, source_target_pairs={{0,16},{16,0},{1,17},{17,1},{2,18},{18,2},{3,19},{19,3},{4,20},{20... | collective-permute-start | bytes 393224 | tf_op jit(solution)/shard_map/ppermute | solution.py:16
  5.6 1.6 %collective-permute-start.3 = (bf16[4,128,128]{2,1,0:T(8,128)(2,1)}, bf16[4,128,128]{2,1,0:T(8,128)(2,1)S(1)}, u32[]{:S(2)}, u32[]{:S(2)}) collective-permute-start(bf16[4,128,128]{2,1,0:T(8,128)(2,1)} %bitcast.14), channel_id=1, source_target_pairs={{0,4},{4,0},{8,12},{12,8},{1,5},{5,1},{9,13},{13,9},{2,6},{6,2},{1... | collective-permute-start | bytes 393224 | tf_op jit(solution)/shard_map/ppermute | solution.py:16
  7.1 3.5 %collective-permute-done.1.refs_2_ = bf16[4,128,128]{2,1,0:T(8,128)(2,1)S(1)} collective-permute-done((bf16[4,128,128]{2,1,0:T(8,128)(2,1)}, bf16[4,128,128]{2,1,0:T(8,128)(2,1)S(1)}, u32[]{:S(2)}, u32[]{:S(2)}) %collective-permute-start.1) | collective-permute-done | bytes 131104 | tf_op jit(solution)/shard_map/ppermute | solution.py:16
  10.7 0.8 %collective-permute-start.2 = (bf16[4,128,128]{2,1,0:T(8,128)(2,1)S(1)}, bf16[4,128,128]{2,1,0:T(8,128)(2,1)S(1)}, u32[]{:S(2)}, u32[]{:S(2)}) collective-permute-start(bf16[4,128,128]{2,1,0:T(8,128)(2,1)S(1)} %collective-permute-done.1.refs_2_), channel_id=1, source_target_pairs={{0,4},{4,0},{8,12},{12,8},{1,5},{5,1},{9,13},{13,9},{2,6},{6,2},{1... | collective-permute-start | bytes 393224 | tf_op jit(solution)/shard_map/ppermute | solution.py:16
  11.4 3.0 %pair_table.1.table = s32[384]{0:T(512)S(4)} custom-call(s32[1,1,1,4,2,4,12]{6,5,4,3,2,1,0:T(4,128)} %lists.1), custom_call_target="tpu_custom_call" | custom-call | tf_op jit(solution)/shard_map/pair_table/pallas_call | solution.py:109
  14.5 0.0 collective-permute-done.refs_1_
  14.5 0.0 copy-start
  14.5 0.9 %copy-done = bf16[1,1,1,4,128,128]{5,4,3,2,1,0:T(8,128)(2,1)S(1)} copy-done((bf16[1,1,1,4,128,128]{5,4,3,2,1,0:T(8,128)(2,1)S(1)}, bf16[1,1,1,4,128,128]{5,4,3,2,1,0:T(8,128)(2,1)}, u32[]{:S(2)}) %copy-start) | copy-done | bytes 131096
  15.4 0.0 collective-permute-done.3.refs_1_
  15.4 1.4 %early_products.1 = (f32[6,128,128]{2,1,0:T(8,128)S(1)}, f32[6,128,128]{2,1,0:T(8,128)S(1)}) custom-call(s32[384]{0:T(512)S(4)} %pair_table.1.table, bf16[9,128,128]{2,1,0:T(8,128)(2,1)S(1)} %right_panel.1.panel, bf16[4,128,128]{2,1,0:T(8,128)(2,1)S(1)} %bitcast.16, bf16[4,128,128]{2,1,0:T(8,128)(2,1)S(1)} %collective-permute-done.3.refs_1_, ...), custom_call_target="tpu_custom_call" | custom-call | flops 603979776 | tf_op jit(solution)/shard_map/early_products/pallas_call | solution.py:131
  16.8 0.0 collective-permute-done.2.refs_0_
  16.8 0.6 %late_products.1 = (f32[6,128,128]{2,1,0:T(8,128)S(1)}, f32[6,128,128]{2,1,0:T(8,128)S(1)}) custom-call(s32[384]{0:T(512)S(4)} %pair_table.1.table, bf16[9,128,128]{2,1,0:T(8,128)(2,1)S(1)} %right_panel.1.panel, bf16[4,128,128]{2,1,0:T(8,128)(2,1)S(1)} %collective-permute-done.2.refs_0_, f32[6,128,128]{2,1,0:T(8,128)S(1)} %get-tuple-element.9.refs_1_, ...), custom_call_target="tpu_custom_call" | custom-call | flops 201326592 | tf_op jit(solution)/shard_map/late_products/pallas_call | solution.py:131
  17.4 0.1 collective-permute-start.4
  17.5 1.7 %collective-permute-done.4 = f32[6,128,128]{2,1,0:T(8,128)S(1)} collective-permute-done((f32[6,128,128]{2,1,0:T(8,128)S(1)}, f32[6,128,128]{2,1,0:T(8,128)S(1)}, u32[]{:S(2)}, u32[]{:S(2)}) %collective-permute-start.4) | collective-permute-done | bytes 393248 | tf_op jit(solution)/shard_map/ppermute | solution.py:16
  19.2 0.1 add.16
  19.3 1.6 %collective-permute-start.5 = (f32[1,3,128,128]{3,2,1,0:T(8,128)S(1)}, f32[1,3,128,128]{3,2,1,0:T(8,128)S(1)}, u32[]{:S(2)}, u32[]{:S(2)}) collective-permute-start(f32[1,3,128,128]{3,2,1,0:T(8,128)S(1)} %slice_bitcast_fusion), channel_id=1, source_target_pairs={{0,2},{1,3},{2,0},{3,1},{4,6},{5,7},{6,4},{7,5},{8,10},{9,11},{10,... | collective-permute-start | bytes 589832 | tf_op jit(solution)/shard_map/ppermute | solution.py:16
  20.8 5.5 %collective-permute-done.5 = f32[1,3,128,128]{3,2,1,0:T(8,128)S(1)} collective-permute-done((f32[1,3,128,128]{3,2,1,0:T(8,128)S(1)}, f32[1,3,128,128]{3,2,1,0:T(8,128)S(1)}, u32[]{:S(2)}, u32[]{:S(2)}) %collective-permute-start.5) | collective-permute-done | bytes 196640 | tf_op jit(solution)/shard_map/ppermute | solution.py:16
  26.3 0.7 %fusion.1 = f32[1,1,3,128,128]{4,3,2,1,0:T(8,128)} fusion(f32[1,3,128,128]{3,2,1,0:T(8,128)S(1)} %collective-permute-done.5, f32[1,2,3,128,128]{4,3,2,1,0:T(8,128)S(1)} %bitcast.18), kind=kLoop, calls=%fused_computation.3 | loop fusion | flops 49152 | bytes 589824 | tf_op jit(solution)/shard_map/reshape | solution.py:155
  (2 shorter events, 0.0 us)
Async XLA Ops:
  0.0 10.7 %collective-permute-start.1 = (bf16[4,128,128]{2,1,0:T(8,128)(2,1)}, bf16[4,128,128]{2,1,0:T(8,128)(2,1)S(1)}, u32[]{:S(2)}, u32[]{:S(2)}) collective-permute-start(bf16[4,128,128]{2,1,0:T(8,128)(2,1)} %bitcast.12), channel_id=1, source_target_pairs={{0,8},{4,12},{8,0},{12,4},{1,9},{5,13},{9,1},{13,5},{2,10},{6,14},... | collective-permute-start | bytes 393224 | tf_op jit(solution)/shard_map/ppermute | solution.py:16
  4.0 10.4 %collective-permute-start = (bf16[4,128,128]{2,1,0:T(8,128)(2,1)}, bf16[4,128,128]{2,1,0:T(8,128)(2,1)S(1)}, u32[]{:S(2)}, u32[]{:S(2)}) collective-permute-start(bf16[4,128,128]{2,1,0:T(8,128)(2,1)} %bitcast.13), channel_id=1, source_target_pairs={{0,16},{16,0},{1,17},{17,1},{2,18},{18,2},{3,19},{19,3},{4,20},{20... | collective-permute-start | bytes 393224 | tf_op jit(solution)/shard_map/ppermute | solution.py:16
  5.6 9.9 %collective-permute-start.3 = (bf16[4,128,128]{2,1,0:T(8,128)(2,1)}, bf16[4,128,128]{2,1,0:T(8,128)(2,1)S(1)}, u32[]{:S(2)}, u32[]{:S(2)}) collective-permute-start(bf16[4,128,128]{2,1,0:T(8,128)(2,1)} %bitcast.14), channel_id=1, source_target_pairs={{0,4},{4,0},{8,12},{12,8},{1,5},{5,1},{9,13},{13,9},{2,6},{6,2},{1... | collective-permute-start | bytes 393224 | tf_op jit(solution)/shard_map/ppermute | solution.py:16
  10.7 6.2 %collective-permute-start.2 = (bf16[4,128,128]{2,1,0:T(8,128)(2,1)S(1)}, bf16[4,128,128]{2,1,0:T(8,128)(2,1)S(1)}, u32[]{:S(2)}, u32[]{:S(2)}) collective-permute-start(bf16[4,128,128]{2,1,0:T(8,128)(2,1)S(1)} %collective-permute-done.1.refs_2_), channel_id=1, source_target_pairs={{0,4},{4,0},{8,12},{12,8},{1,5},{5,1},{9,13},{13,9},{2,6},{6,2},{1... | collective-permute-start | bytes 393224 | tf_op jit(solution)/shard_map/ppermute | solution.py:16
  14.5 0.9 %copy-start = (bf16[1,1,1,4,128,128]{5,4,3,2,1,0:T(8,128)(2,1)S(1)}, bf16[1,1,1,4,128,128]{5,4,3,2,1,0:T(8,128)(2,1)}, u32[]{:S(2)}) copy-start(bf16[1,1,1,4,128,128]{5,4,3,2,1,0:T(8,128)(2,1)} %param.2) | copy-start | bytes 393220
  17.4 1.8 %collective-permute-start.4 = (f32[6,128,128]{2,1,0:T(8,128)S(1)}, f32[6,128,128]{2,1,0:T(8,128)S(1)}, u32[]{:S(2)}, u32[]{:S(2)}) collective-permute-start(f32[6,128,128]{2,1,0:T(8,128)S(1)} %get-tuple-element.12), channel_id=1, source_target_pairs={{0,1},{1,0},{2,3},{3,2},{4,5},{5,4},{6,7},{7,6},{8,9},{9,8},{10,11... | collective-permute-start | bytes 1179656 | tf_op jit(solution)/shard_map/ppermute | solution.py:16
  19.3 7.0 %collective-permute-start.5 = (f32[1,3,128,128]{3,2,1,0:T(8,128)S(1)}, f32[1,3,128,128]{3,2,1,0:T(8,128)S(1)}, u32[]{:S(2)}, u32[]{:S(2)}) collective-permute-start(f32[1,3,128,128]{3,2,1,0:T(8,128)S(1)} %slice_bitcast_fusion), channel_id=1, source_target_pairs={{0,2},{1,3},{2,0},{3,1},{4,6},{5,7},{6,4},{7,5},{8,10},{9,11},{10,... | collective-permute-start | bytes 589832 | tf_op jit(solution)/shard_map/ppermute | solution.py:16

commit v2 on v0

v2 whole, which is shorter than its diff:
```python
import functools

import jax
import jax.numpy as jnp
from jax import lax
from jax.experimental import pallas as pl
from jax.experimental.pallas import tpu as pltpu
from jax.sharding import PartitionSpec as P

VMEM = pl.BlockSpec(memory_space=pltpu.VMEM)
SMEM = pl.BlockSpec(memory_space=pltpu.SMEM)
ANY = pl.BlockSpec(memory_space=pl.ANY)
WEIGHT = 20


def exchange(block, axis, distance):
    size = lax.axis_size(axis)
    return lax.ppermute(block, axis, [(i, i ^ distance) for i in range(size)])


def ring_place(index, size):
    return jnp.where(index % 2 == 0, index // 2, size - (index + 1) // 2)


def ring_device(place, size):
    return jnp.where(place < (size + 1) // 2, 2 * place, 2 * (size - place) - 1)


def turn(block, axis, step):
    size = lax.axis_size(axis)
    ring = [*range(0, size, 2), *reversed(range(1, size, 2))]
    return lax.ppermute(block, axis, [(ring[i], ring[(i + step) % size]) for i in range(size)])


def in_vmem(x):
    return pltpu.with_memory_space_constraint(x, pltpu.VMEM)


def lists_kernel(lists, held, sem):
    copy = pltpu.make_async_copy(lists, held, sem)
    copy.start()
    copy.wait()


def panel_kernel(lists, *refs):
    sources, panel = refs[:-1], refs[-1]
    slots = sources[0].shape[0]
    row = lax.axis_index("row")
    for hop, source in enumerate(sources):
        panel[pl.ds((row ^ hop) * slots, slots)] = source[...]
    panel[len(sources) * slots] = jnp.zeros(panel.shape[1:], panel.dtype)


def add_kernel(steps, groups, started, lists, panel, *refs):
    lefts, refs = refs[: len(steps)], refs[len(steps) :]
    sources, targets = (refs[: len(groups)], refs[len(groups) :]) if started else (None, refs)
    cols, pairs = lists.shape[3], lists.shape[5]
    slots = lefts[0].shape[0]
    zero_slot = panel.shape[0] - 1
    share = targets[0].shape[0]
    col, layer = lax.axis_index("col"), lax.axis_index("depth")
    width = 2 if pairs % 2 == 0 else 1

    def products(step, left, out):
        place = lax.rem(ring_place(col, cols) - step + cols, cols)
        shift = lax.rem(col - ring_device(place, cols) + cols, cols)
        total = None
        for m in range(0, pairs, width):
            chosen, partner = [], []
            for j in range(m, m + width):
                slot = lists[0, 0, 0, shift, 0, j, out]
                live = slot < slots
                chosen.append(left[jnp.where(live, slot, 0)])
                partner.append(panel[jnp.where(live, lists[0, 0, 0, shift, 1, j, out], zero_slot)])
            term = lax.dot_general(
                jnp.concatenate(chosen, 1),
                jnp.concatenate(partner, 1),
                (((1,), (1,)), ((), ())),
                preferred_element_type=jnp.float32,
            )
            total = term if total is None else total + term
        return total

    for k, group in enumerate(groups):
        for i in range(share):
            out = (layer ^ group) * share + i
            total = sources[k][i] if started else None
            for step, left in zip(steps, lefts):
                term = products(step, left, out)
                total = term if total is None else total + term
            targets[k][i] = total


def body(a_tiles, pair_lists):
    rows, cols, depths = (lax.axis_size(name) for name in ("row", "col", "depth"))
    slots, width = a_tiles.shape[3], a_tiles.shape[4]
    pairs, outs = pair_lists.shape[5:]
    share = outs // depths
    own = a_tiles.reshape(slots, width, width)

    lefts = {0: own}
    for step in range(1, cols // 2 + 1):
        lefts[step] = turn(lefts[step - 1], "col", 1)
        if 2 * step < cols:
            lefts[-step] = turn(lefts[1 - step], "col", -1)
    rights = {0: own}
    for bit in [1 << b for b in range(rows.bit_length() - 1)]:
        rights.update({hop ^ bit: exchange(block, "row", bit) for hop, block in list(rights.items())})

    lists = pl.pallas_call(
        lists_kernel,
        out_shape=pltpu.SMEM(pair_lists.shape, jnp.int32),
        in_specs=[ANY],
        out_specs=SMEM,
        scratch_shapes=[pltpu.SemaphoreType.DMA],
        name="pair_lists",
    )(pair_lists)
    lists = pltpu.with_memory_space_constraint(lists, pltpu.SMEM)
    panel = pl.pallas_call(
        panel_kernel,
        out_shape=pltpu.VMEM((rows * slots + 1, width, width), a_tiles.dtype),
        in_specs=[SMEM] + [VMEM] * rows,
        out_specs=VMEM,
        name="right_panel",
    )(lists, *[in_vmem(rights[i]) for i in range(rows)])

    def add(steps, groups, sums, name):
        started = [sums[g] for g in groups if g in sums]
        flops = 2 * width**3 * pairs * share * len(groups) * len(steps)
        totals = pl.pallas_call(
            functools.partial(add_kernel, steps, groups, bool(started)),
            out_shape=[pltpu.VMEM((share, width, width), jnp.float32)] * len(groups),
            in_specs=[SMEM] + [VMEM] * (1 + len(steps) + len(started)),
            out_specs=[VMEM] * len(groups),
            name=name,
            cost_estimate=pl.CostEstimate(
                flops=WEIGHT * flops, bytes_accessed=0, transcendentals=0
            ),
        )(lists, in_vmem(panel), *[in_vmem(lefts[s]) for s in steps], *[in_vmem(s) for s in started])
        return dict(zip(groups, totals))

    last = cols // 2
    early = [s for s in lefts if s != last]
    near, far = [0, 1], list(range(2, depths))
    sums = add(early, far + near, {}, "early_products")
    if far:
        sums.update(add([last], far, sums, "late_products_far"))
    sums.update(add([last], near, sums, "late_products_near"))

    bit = 1
    while bit < depths:
        for group in reversed([g for g in sums if not g & bit]):
            sums[group] = sums[group] + exchange(sums.pop(group | bit), "depth", bit)
        bit *= 2
    return sums[0].reshape(1, 1, share, width, width)


def solution(mesh):
    placed = (
        P("row", "col", "depth", None, None, None),
        P("row", "col", "depth", None, None, None, None),
    )
    return jax.shard_map(
        body,
        mesh=mesh,
        in_specs=placed,
        out_specs=P("row", "col", "depth", None, None),
        check_vma=False,
    )
```

time: 84.3 us -> 24.3 us (0.29)
  waiting for transfers between devices: 34.4 us -> 8.2 us
  local copies, waits for them, and re-layouts: 15.2 us -> 0.9 us
  between operations: 13.4 us -> 0.06 us
  starting transfers between devices: 1.84 us -> 11 us
  matrix products: 8.18 us -> 0 us
  blocking collectives: 7.12 us -> 0 us
  Pallas kernels: 0 us -> 3.19 us
  other arithmetic: 3.57 us -> 0.73 us
    reduce_scatter x1 -> x0, waiting for transfers between devices: 21.9 us -> none  [body(): lax.psum_scatter(running, 'depth', scatter_dimension=0, tiled=True)]
    gather x8 -> x0, local copies, waits for them, and re-layouts: 10.1 us -> none  [the longest x4 6.69 us: contract(): chosen = jnp.take(left_set, left_index, axis=0)]
    ppermute x3 -> x7, starting transfers between devices: 1.83 us -> 11 us  [the longest x3 7.31 us: turn(): lax.ppermute(block, axis, [(ring[i], ring[(i + step) % size]) for i in ra...]
    dot_general x4 -> x0, matrix products: 8.18 us -> none  [contract(): jnp.einsum('moik,mojk->oij', chosen, partner, preferred_element_type=jnp....]
    all_gather x1 -> x0, blocking collectives: 7.12 us -> none  [body(): right_panel = lax.all_gather(own_tiles, 'row', axis=0, tiled=True)]
    ppermute x3 -> x7, waiting for transfers between devices: 12.6 us -> 8.2 us  [the longest x4 5.95 us: exchange(): return lax.ppermute(block, axis, [(i, i ^ distance) for i in range(size)])]
    pallas_call x0 -> x5, Pallas kernels: none -> 3.19 us  [the longest x3 2.22 us: add(): pl.pallas_call(functools.partial(add_kernel, steps, groups, bool(started)...]
    and x4 -> x0, other arithmetic: 2.82 us -> none  [contract(): chosen = jnp.take(left_set, left_index, axis=0)]
  transfers between devices with their start and end apart: 4 -> 7, of which waited for: 4 -> 4; matrix products, arithmetic and copies ran while one was open for 7% -> 0% of each run, Pallas kernels for 0% -> 12%
where the time goes in v2:
time: 24.3 us; the launch traced here: 24.1 us
  starting transfers between devices  11 us (45%)
  waiting for transfers between devices  8.2 us (34%)
  Pallas kernels  3.19 us (13%)
  local copies, waits for them, and re-layouts  0.9 us (4%)
  other arithmetic  0.73 us (3%)
    ppermute x3, starting transfers between devices, turn(): lax.ppermute(block, axis, [(ring[i], ring[(i + step) % size]) for i in ra...  7.31 us
    ppermute x4, waiting for transfers between devices, exchange(): return lax.ppermute(block, axis, [(i, i ^ distance) for i in range(size)])  5.95 us
    ppermute x4, starting transfers between devices, exchange(): return lax.ppermute(block, axis, [(i, i ^ distance) for i in range(size)])  3.66 us
    ppermute x3, waiting for transfers between devices, turn(): lax.ppermute(block, axis, [(ring[i], ring[(i + step) % size]) for i in ra...  2.25 us
    pallas_call x3, Pallas kernels, add(): pl.pallas_call(functools.partial(add_kernel, steps, groups, bool(started)...  2.22 us
    pallas_call x1, Pallas kernels, body(): pl.pallas_call(lists_kernel, out_shape=pltpu.SMEM(pair_lists.shape, jnp.i...  0.93 us
    unnamed x2, local copies, waits for them, and re-layouts  0.9 us
    reshape x1, other arithmetic, body(): return sums[0].reshape(1, 1, share, width, width)  0.71 us
  transfers between devices with their start and end apart: 7, of which 4 were waited for; matrix products, arithmetic and copies ran while one was open for 0% of the time, Pallas kernels for 12%

profile of v2, /device:TPU:0, one launch (start us, length us, event | category | flops | bytes accessed | tf_op | source)
XLA Modules:
  0.0 24.1 jit_solution(14641615155769874006)
XLA Ops:
  0.0 4.0 %collective-permute-start.1 = (bf16[4,128,128]{2,1,0:T(8,128)(2,1)}, bf16[4,128,128]{2,1,0:T(8,128)(2,1)S(1)}, u32[]{:S(2)}, u32[]{:S(2)}) collective-permute-start(bf16[4,128,128]{2,1,0:T(8,128)(2,1)} %bitcast.3), channel_id=1, source_target_pairs={{0,8},{8,12},{12,4},{4,0},{1,9},{9,13},{13,5},{5,1},{2,10},{10,14}... | collective-permute-start | bytes 393224 | tf_op jit(solution)/shard_map/ppermute | solution.py:32
  4.0 1.5 %collective-permute-start = (bf16[4,128,128]{2,1,0:T(8,128)(2,1)}, bf16[4,128,128]{2,1,0:T(8,128)(2,1)S(1)}, u32[]{:S(2)}, u32[]{:S(2)}) collective-permute-start(bf16[4,128,128]{2,1,0:T(8,128)(2,1)} %bitcast.4), channel_id=1, source_target_pairs={{0,16},{16,0},{1,17},{17,1},{2,18},{18,2},{3,19},{19,3},{4,20},{20... | collective-permute-start | bytes 393224 | tf_op jit(solution)/shard_map/ppermute | solution.py:18
  5.6 0.0 collective-permute-start.3
  5.6 0.9 %pair_lists.1.lists = s32[1,1,1,4,2,4,12]{6,5,4,3,2,1,0:T(4,128)S(4)} custom-call(s32[1,1,1,4,2,4,12]{6,5,4,3,2,1,0:T(4,128)} %lists.1), custom_call_target="tpu_custom_call" | custom-call | tf_op jit(solution)/shard_map/pair_lists/pallas_call | solution.py:110
  6.5 1.8 %collective-permute-done.1.refs_1_ = bf16[4,128,128]{2,1,0:T(8,128)(2,1)S(1)} collective-permute-done((bf16[4,128,128]{2,1,0:T(8,128)(2,1)}, bf16[4,128,128]{2,1,0:T(8,128)(2,1)S(1)}, u32[]{:S(2)}, u32[]{:S(2)}) %collective-permute-start.1) | collective-permute-done | bytes 131104 | tf_op jit(solution)/shard_map/ppermute | solution.py:32
  8.3 3.3 %collective-permute-start.2 = (bf16[4,128,128]{2,1,0:T(8,128)(2,1)S(1)}, bf16[4,128,128]{2,1,0:T(8,128)(2,1)S(1)}, u32[]{:S(2)}, u32[]{:S(2)}) collective-permute-start(bf16[4,128,128]{2,1,0:T(8,128)(2,1)S(1)} %collective-permute-done.1.refs_1_), channel_id=1, source_target_pairs={{0,8},{8,12},{12,4},{4,0},{1,9},{9,13},{13,5},{5,1},{2,10},{10,14}... | collective-permute-start | bytes 393224 | tf_op jit(solution)/shard_map/ppermute | solution.py:32
  11.5 0.0 collective-permute-done.refs_1_
  11.5 0.0 copy-start
  11.5 0.9 %copy-done = bf16[1,1,1,4,128,128]{5,4,3,2,1,0:T(8,128)(2,1)S(1)} copy-done((bf16[1,1,1,4,128,128]{5,4,3,2,1,0:T(8,128)(2,1)S(1)}, bf16[1,1,1,4,128,128]{5,4,3,2,1,0:T(8,128)(2,1)}, u32[]{:S(2)}) %copy-start) | copy-done | bytes 131096
  12.5 0.0 collective-permute-done.3.refs_2_
  12.5 1.4 %early_products.1 = (f32[3,128,128]{2,1,0:T(8,128)S(1)}, f32[3,128,128]{2,1,0:T(8,128)S(1)}, f32[3,128,128]{2,1,0:T(8,128)S(1)}, f32[3,128,128]{2,1,0:T(8,128)S(1)}) custom-call(s32[1,1,1,4,2,4,12]{6,5,4,3,2,1,0:T(4,128)S(4)} %pair_lists.1.lists, bf16[9,128,128]{2,1,0:T(8,128)(2,1)S(1)} %right_panel.1.panel, bf16[4,128,128]{2,1,0:T(8,128)(2,1)S(1)} %bitcast.7, ...), custom_call_target="tpu_custom_call" | custom-call | flops 12079595520 | tf_op jit(solution)/shard_map/early_products/pallas_call | solution.py:130
  13.9 0.5 %collective-permute-done.2.refs_0_ = bf16[4,128,128]{2,1,0:T(8,128)(2,1)S(1)} collective-permute-done((bf16[4,128,128]{2,1,0:T(8,128)(2,1)S(1)}, bf16[4,128,128]{2,1,0:T(8,128)(2,1)S(1)}, u32[]{:S(2)}, u32[]{:S(2)}) %collective-permute-start.2) | collective-permute-done | bytes 131104 | tf_op jit(solution)/shard_map/ppermute | solution.py:32
  14.4 0.4 %late_products_far.1 = (f32[3,128,128]{2,1,0:T(8,128)S(1)}, f32[3,128,128]{2,1,0:T(8,128)S(1)}) custom-call(s32[1,1,1,4,2,4,12]{6,5,4,3,2,1,0:T(4,128)S(4)} %pair_lists.1.lists, bf16[9,128,128]{2,1,0:T(8,128)(2,1)S(1)} %right_panel.1.panel, bf16[4,128,128]{2,1,0:T(8,128)(2,1)S(1)} %collective-permute-done.2.refs_0_, ...), custom_call_target="tpu_custom_call" | custom-call | flops 2013265920 | tf_op jit(solution)/shard_map/late_products_far/pallas_call | solution.py:130
  14.8 0.1 collective-permute-start.5
  14.9 0.4 %late_products_near.1 = (f32[3,128,128]{2,1,0:T(8,128)S(1)}, f32[3,128,128]{2,1,0:T(8,128)S(1)}) custom-call(s32[1,1,1,4,2,4,12]{6,5,4,3,2,1,0:T(4,128)S(4)} %pair_lists.1.lists, bf16[9,128,128]{2,1,0:T(8,128)(2,1)S(1)} %right_panel.1.panel, bf16[4,128,128]{2,1,0:T(8,128)(2,1)S(1)} %collective-permute-done.2.refs_0_, ...), custom_call_target="tpu_custom_call" | custom-call | flops 2013265920 | tf_op jit(solution)/shard_map/late_products_near/pallas_call | solution.py:130
  15.3 0.5 %collective-permute-start.4 = (f32[3,128,128]{2,1,0:T(8,128)S(1)}, f32[3,128,128]{2,1,0:T(8,128)S(1)}, u32[]{:S(2)}, u32[]{:S(2)}) collective-permute-start(f32[3,128,128]{2,1,0:T(8,128)S(1)} %get-tuple-element.16), channel_id=1, source_target_pairs={{0,1},{1,0},{2,3},{3,2},{4,5},{5,4},{6,7},{7,6},{8,9},{9,8},{10,11... | collective-permute-start | bytes 589832 | tf_op jit(solution)/shard_map/ppermute | solution.py:18
  15.8 0.5 %collective-permute-done.5 = f32[3,128,128]{2,1,0:T(8,128)S(1)} collective-permute-done((f32[3,128,128]{2,1,0:T(8,128)S(1)}, f32[3,128,128]{2,1,0:T(8,128)S(1)}, u32[]{:S(2)}, u32[]{:S(2)}) %collective-permute-start.5) | collective-permute-done | bytes 196640 | tf_op jit(solution)/shard_map/ppermute | solution.py:18
  16.3 1.6 %collective-permute-start.6 = (f32[3,128,128]{2,1,0:T(8,128)S(1)}, f32[3,128,128]{2,1,0:T(8,128)S(1)}, u32[]{:S(2)}, u32[]{:S(2)}) collective-permute-start(f32[3,128,128]{2,1,0:T(8,128)S(1)} %add.10), channel_id=1, source_target_pairs={{0,2},{1,3},{2,0},{3,1},{4,6},{5,7},{6,4},{7,5},{8,10},{9,11},{10,... | collective-permute-start | bytes 589832 | tf_op jit(solution)/shard_map/ppermute | solution.py:18
  17.9 0.0 collective-permute-done.4
  17.9 5.5 %collective-permute-done.6 = f32[3,128,128]{2,1,0:T(8,128)S(1)} collective-permute-done((f32[3,128,128]{2,1,0:T(8,128)S(1)}, f32[3,128,128]{2,1,0:T(8,128)S(1)}, u32[]{:S(2)}, u32[]{:S(2)}) %collective-permute-start.6) | collective-permute-done | bytes 196640 | tf_op jit(solution)/shard_map/ppermute | solution.py:18
  23.3 0.7 %add_bitcast_fusion = f32[1,1,3,128,128]{4,3,2,1,0:T(8,128)} fusion(f32[3,128,128]{2,1,0:T(8,128)S(1)} %collective-permute-done.6, f32[3,128,128]{2,1,0:T(8,128)S(1)} %get-tuple-element.15, f32[3,128,128]{2,1,0:T(8,128)S(1)} %collective-permute-done.4), kind=kLoop, calls=%fused_computation | loop fusion | flops 98304 | bytes 786432 | tf_op jit(solution)/shard_map/reshape | solution.py:155
  (2 shorter events, 0.1 us)
Async XLA Ops:
  0.0 8.3 %collective-permute-start.1 = (bf16[4,128,128]{2,1,0:T(8,128)(2,1)}, bf16[4,128,128]{2,1,0:T(8,128)(2,1)S(1)}, u32[]{:S(2)}, u32[]{:S(2)}) collective-permute-start(bf16[4,128,128]{2,1,0:T(8,128)(2,1)} %bitcast.3), channel_id=1, source_target_pairs={{0,8},{8,12},{12,4},{4,0},{1,9},{9,13},{13,5},{5,1},{2,10},{10,14}... | collective-permute-start | bytes 393224 | tf_op jit(solution)/shard_map/ppermute | solution.py:32
  4.0 7.5 %collective-permute-start = (bf16[4,128,128]{2,1,0:T(8,128)(2,1)}, bf16[4,128,128]{2,1,0:T(8,128)(2,1)S(1)}, u32[]{:S(2)}, u32[]{:S(2)}) collective-permute-start(bf16[4,128,128]{2,1,0:T(8,128)(2,1)} %bitcast.4), channel_id=1, source_target_pairs={{0,16},{16,0},{1,17},{17,1},{2,18},{18,2},{3,19},{19,3},{4,20},{20... | collective-permute-start | bytes 393224 | tf_op jit(solution)/shard_map/ppermute | solution.py:18
  5.6 6.9 %collective-permute-start.3 = (bf16[4,128,128]{2,1,0:T(8,128)(2,1)}, bf16[4,128,128]{2,1,0:T(8,128)(2,1)S(1)}, u32[]{:S(2)}, u32[]{:S(2)}) collective-permute-start(bf16[4,128,128]{2,1,0:T(8,128)(2,1)} %bitcast.5), channel_id=1, source_target_pairs={{0,4},{8,0},{12,8},{4,12},{1,5},{9,1},{13,9},{5,13},{2,6},{10,2},{... | collective-permute-start | bytes 393224 | tf_op jit(solution)/shard_map/ppermute | solution.py:32
  8.3 6.2 %collective-permute-start.2 = (bf16[4,128,128]{2,1,0:T(8,128)(2,1)S(1)}, bf16[4,128,128]{2,1,0:T(8,128)(2,1)S(1)}, u32[]{:S(2)}, u32[]{:S(2)}) collective-permute-start(bf16[4,128,128]{2,1,0:T(8,128)(2,1)S(1)} %collective-permute-done.1.refs_1_), channel_id=1, source_target_pairs={{0,8},{8,12},{12,4},{4,0},{1,9},{9,13},{13,5},{5,1},{2,10},{10,14}... | collective-permute-start | bytes 393224 | tf_op jit(solution)/shard_map/ppermute | solution.py:32
  11.5 0.9 %copy-start = (bf16[1,1,1,4,128,128]{5,4,3,2,1,0:T(8,128)(2,1)S(1)}, bf16[1,1,1,4,128,128]{5,4,3,2,1,0:T(8,128)(2,1)}, u32[]{:S(2)}) copy-start(bf16[1,1,1,4,128,128]{5,4,3,2,1,0:T(8,128)(2,1)} %param.2) | copy-start | bytes 393220
  14.8 1.5 %collective-permute-start.5 = (f32[3,128,128]{2,1,0:T(8,128)S(1)}, f32[3,128,128]{2,1,0:T(8,128)S(1)}, u32[]{:S(2)}, u32[]{:S(2)}) collective-permute-start(f32[3,128,128]{2,1,0:T(8,128)S(1)} %get-tuple-element.20), channel_id=1, source_target_pairs={{0,1},{1,0},{2,3},{3,2},{4,5},{5,4},{6,7},{7,6},{8,9},{9,8},{10,11... | collective-permute-start | bytes 589832 | tf_op jit(solution)/shard_map/ppermute | solution.py:18
  15.3 2.6 %collective-permute-start.4 = (f32[3,128,128]{2,1,0:T(8,128)S(1)}, f32[3,128,128]{2,1,0:T(8,128)S(1)}, u32[]{:S(2)}, u32[]{:S(2)}) collective-permute-start(f32[3,128,128]{2,1,0:T(8,128)S(1)} %get-tuple-element.16), channel_id=1, source_target_pairs={{0,1},{1,0},{2,3},{3,2},{4,5},{5,4},{6,7},{7,6},{8,9},{9,8},{10,11... | collective-permute-start | bytes 589832 | tf_op jit(solution)/shard_map/ppermute | solution.py:18
  16.3 7.0 %collective-permute-start.6 = (f32[3,128,128]{2,1,0:T(8,128)S(1)}, f32[3,128,128]{2,1,0:T(8,128)S(1)}, u32[]{:S(2)}, u32[]{:S(2)}) collective-permute-start(f32[3,128,128]{2,1,0:T(8,128)S(1)} %add.10), channel_id=1, source_target_pairs={{0,2},{1,3},{2,0},{3,1},{4,6},{5,7},{6,4},{7,5},{8,10},{9,11},{10,... | collective-permute-start | bytes 589832 | tf_op jit(solution)/shard_map/ppermute | solution.py:18

commit v3 on v2

--- a/solution.py
+++ b/solution.py
@@ -36,14 +36,19 @@
     return pltpu.with_memory_space_constraint(x, pltpu.VMEM)
 
 
-def lists_kernel(lists, held, sem):
-    copy = pltpu.make_async_copy(lists, held, sem)
-    copy.start()
-    copy.wait()
+def stage_kernel(tiles, lists, held, own, sems):
+    copies = [
+        pltpu.make_async_copy(lists, held, sems.at[0]),
+        pltpu.make_async_copy(tiles, own, sems.at[1]),
+    ]
+    for copy in copies:
+        copy.start()
+    for copy in copies:
+        copy.wait()
 
 
-def panel_kernel(lists, *refs):
-    sources, panel = refs[:-1], refs[-1]
+def panel_kernel(*refs):
+    *sources, _, panel = refs
     slots = sources[0].shape[0]
     row = lax.axis_index("row")
     for hop, source in enumerate(sources):
@@ -96,63 +101,65 @@
     slots, width = a_tiles.shape[3], a_tiles.shape[4]
     pairs, outs = pair_lists.shape[5:]
     share = outs // depths
-    own = a_tiles.reshape(slots, width, width)
+    tiles = a_tiles.reshape(slots, width, width)
 
-    lefts = {0: own}
-    for step in range(1, cols // 2 + 1):
+    lists, own = pl.pallas_call(
+        stage_kernel,
+        out_shape=(
+            pltpu.SMEM(pair_lists.shape, jnp.int32),
+            pltpu.VMEM(tiles.shape, tiles.dtype),
+        ),
+        in_specs=[ANY, ANY],
+        out_specs=(SMEM, VMEM),
+        scratch_shapes=[pltpu.SemaphoreType.DMA((2,))],
+        name="stage",
+    )(tiles, pair_lists)
+    lists = pltpu.with_memory_space_constraint(lists, pltpu.SMEM)
+
+    last = cols // 2
+    lefts = {0: tiles}
+    for step in range(1, last + 1):
         lefts[step] = turn(lefts[step - 1], "col", 1)
-        if 2 * step < cols:
-            lefts[-step] = turn(lefts[1 - step], "col", -1)
-    rights = {0: own}
+    for step in range(1, (cols + 1) // 2):
+        lefts[-step] = turn(lefts[1 - step], "col", -1)
+    rights = {0: tiles}
     for bit in [1 << b for b in range(rows.bit_length() - 1)]:
         rights.update({hop ^ bit: exchange(block, "row", bit) for hop, block in list(rights.items())})
+    lefts[0] = rights[0] = own
 
-    lists = pl.pallas_call(
-        lists_kernel,
-        out_shape=pltpu.SMEM(pair_lists.shape, jnp.int32),
-        in_specs=[ANY],
-        out_specs=SMEM,
-        scratch_shapes=[pltpu.SemaphoreType.DMA],
-        name="pair_lists",
-    )(pair_lists)
-    lists = pltpu.with_memory_space_constraint(lists, pltpu.SMEM)
     panel = pl.pallas_call(
         panel_kernel,
         out_shape=pltpu.VMEM((rows * slots + 1, width, width), a_tiles.dtype),
-        in_specs=[SMEM] + [VMEM] * rows,
+        in_specs=[VMEM] * (1 + rows),
         out_specs=VMEM,
         name="right_panel",
-    )(lists, *[in_vmem(rights[i]) for i in range(rows)])
+    )(*[in_vmem(rights[i]) for i in range(rows)], in_vmem(lefts[min(lefts)]))
+
+    block = pltpu.VMEM((share, width, width), jnp.float32)
 
     def add(steps, groups, sums, name):
-        started = [sums[g] for g in groups if g in sums]
         flops = 2 * width**3 * pairs * share * len(groups) * len(steps)
-        totals = pl.pallas_call(
-            functools.partial(add_kernel, steps, groups, bool(started)),
-            out_shape=[pltpu.VMEM((share, width, width), jnp.float32)] * len(groups),
-            in_specs=[SMEM] + [VMEM] * (1 + len(steps) + len(started)),
-            out_specs=[VMEM] * len(groups),
-            name=name,
-            cost_estimate=pl.CostEstimate(
-                flops=WEIGHT * flops, bytes_accessed=0, transcendentals=0
-            ),
-        )(lists, in_vmem(panel), *[in_vmem(lefts[s]) for s in steps], *[in_vmem(s) for s in started])
-        return dict(zip(groups, totals))
+        return list(
+            pl.pallas_call(
+                functools.partial(add_kernel, steps, groups, bool(sums)),
+                out_shape=[block] * len(groups),
+                in_specs=[SMEM] + [VMEM] * (1 + len(steps) + len(sums)),
+                out_specs=[VMEM] * len(groups),
+                name=name,
+                cost_estimate=pl.CostEstimate(
+                    flops=WEIGHT * flops, bytes_accessed=0, transcendentals=0
+                ),
+            )(lists, in_vmem(panel), *[in_vmem(lefts[s]) for s in steps], *[in_vmem(s) for s in sums])
+        )
 
-    last = cols // 2
-    early = [s for s in lefts if s != last]
-    near, far = [0, 1], list(range(2, depths))
-    sums = add(early, far + near, {}, "early_products")
-    if far:
-        sums.update(add([last], far, sums, "late_products_far"))
-    sums.update(add([last], near, sums, "late_products_near"))
-
-    bit = 1
-    while bit < depths:
-        for group in reversed([g for g in sums if not g & bit]):
-            sums[group] = sums[group] + exchange(sums.pop(group | bit), "depth", bit)
-        bit *= 2
-    return sums[0].reshape(1, 1, share, width, width)
+    sums = add([s for s in lefts if s != last], [2, 3, 0, 1], [], "early_products")
+    far_kept, far_sent = add([last], [2, 3], sums[:2], "late_products_far")
+    near_kept, near_sent = add([last], [0, 1], sums[2:], "late_products_near")
+    far_came = exchange(far_sent, "depth", 1)
+    near_came = exchange(near_sent, "depth", 1)
+    far = far_kept + far_came
+    near = near_kept + near_came
+    return (near + exchange(far, "depth", 2)).reshape(1, 1, share, width, width)
 
 
 def solution(mesh):

time: 24.3 us -> 23.9 us (0.984)
  local copies, waits for them, and re-layouts: 0.9 us -> 0 us
  waiting for transfers between devices: 8.2 us -> 8.71 us
    unnamed x2 -> x0, local copies, waits for them, and re-layouts: 0.9 us -> none
    ppermute x3, waiting for transfers between devices: 2.25 us -> 2.77 us  [turn(): lax.ppermute(block, axis, [(ring[i], ring[(i + step) % size]) for i in ra...]
  transfers between devices with their start and end apart: 7 -> 7, of which waited for: 4 -> 5; matrix products, arithmetic and copies ran while one was open for 0% -> 0% of each run, Pallas kernels for 12% -> 12%
where the time goes in v3:
time: 23.9 us; the launch traced here: 23.7 us
  starting transfers between devices  11 us (46%)
  waiting for transfers between devices  8.71 us (36%)
  Pallas kernels  3.2 us (13%)
  other arithmetic  0.73 us (3%)
    ppermute x3, starting transfers between devices, turn(): lax.ppermute(block, axis, [(ring[i], ring[(i + step) % size]) for i in ra...  7.31 us
    ppermute x4, waiting for transfers between devices, exchange(): return lax.ppermute(block, axis, [(i, i ^ distance) for i in range(size)])  5.94 us
    ppermute x4, starting transfers between devices, exchange(): return lax.ppermute(block, axis, [(i, i ^ distance) for i in range(size)])  3.67 us
    ppermute x3, waiting for transfers between devices, turn(): lax.ppermute(block, axis, [(ring[i], ring[(i + step) % size]) for i in ra...  2.77 us
    pallas_call x3, Pallas kernels, add(): pl.pallas_call(functools.partial(add_kernel, steps, groups, bool(sums)),...  2.22 us
    pallas_call x1, Pallas kernels, body(): pl.pallas_call(stage_kernel, out_shape=(pltpu.SMEM(pair_lists.shape, jnp....  0.95 us
    reshape x1, other arithmetic, body(): return (near + exchange(far, 'depth', 2)).reshape(1, 1, share, width, width)  0.71 us
  transfers between devices with their start and end apart: 7, of which 5 were waited for; matrix products, arithmetic and copies ran while one was open for 0% of the time, Pallas kernels for 12%

profile of v3, /device:TPU:0, one launch (start us, length us, event | category | flops | bytes accessed | tf_op | source)
XLA Modules:
  0.0 23.7 jit_solution(11843030193569209966)
XLA Ops:
  0.0 4.0 %collective-permute-start.2 = (bf16[4,128,128]{2,1,0:T(8,128)(2,1)}, bf16[4,128,128]{2,1,0:T(8,128)(2,1)S(1)}, u32[]{:S(2)}, u32[]{:S(2)}) collective-permute-start(bf16[4,128,128]{2,1,0:T(8,128)(2,1)} %bitcast.3), channel_id=1, source_target_pairs={{0,8},{8,12},{12,4},{4,0},{1,9},{9,13},{13,5},{5,1},{2,10},{10,14}... | collective-permute-start | bytes 393224 | tf_op jit(solution)/shard_map/ppermute | solution.py:32
  4.0 0.0 collective-permute-start.1
  4.0 1.5 %collective-permute-start = (bf16[4,128,128]{2,1,0:T(8,128)(2,1)}, bf16[4,128,128]{2,1,0:T(8,128)(2,1)S(1)}, u32[]{:S(2)}, u32[]{:S(2)}) collective-permute-start(bf16[4,128,128]{2,1,0:T(8,128)(2,1)} %bitcast.5), channel_id=1, source_target_pairs={{0,16},{16,0},{1,17},{17,1},{2,18},{18,2},{3,19},{19,3},{4,20},{20... | collective-permute-start | bytes 393224 | tf_op jit(solution)/shard_map/ppermute | solution.py:18
  5.6 1.0 %stage.1 = (s32[1,1,1,4,2,4,12]{6,5,4,3,2,1,0:T(4,128)S(4)}, bf16[4,128,128]{2,1,0:T(8,128)(2,1)S(1)}) custom-call(bf16[4,128,128]{2,1,0:T(8,128)(2,1)} %bitcast.6, s32[1,1,1,4,2,4,12]{6,5,4,3,2,1,0:T(4,128)} %lists.1), custom_call_target="tpu_custom_call" | custom-call | tf_op jit(solution)/shard_map/stage/pallas_call | solution.py:106
  6.5 1.7 %collective-permute-done.2.refs_1_ = bf16[4,128,128]{2,1,0:T(8,128)(2,1)S(1)} collective-permute-done((bf16[4,128,128]{2,1,0:T(8,128)(2,1)}, bf16[4,128,128]{2,1,0:T(8,128)(2,1)S(1)}, u32[]{:S(2)}, u32[]{:S(2)}) %collective-permute-start.2) | collective-permute-done | bytes 131104 | tf_op jit(solution)/shard_map/ppermute | solution.py:32
  8.3 3.3 %collective-permute-start.3 = (bf16[4,128,128]{2,1,0:T(8,128)(2,1)S(1)}, bf16[4,128,128]{2,1,0:T(8,128)(2,1)S(1)}, u32[]{:S(2)}, u32[]{:S(2)}) collective-permute-start(bf16[4,128,128]{2,1,0:T(8,128)(2,1)S(1)} %collective-permute-done.2.refs_1_), channel_id=1, source_target_pairs={{0,8},{8,12},{12,4},{4,0},{1,9},{9,13},{13,5},{5,1},{2,10},{10,14}... | collective-permute-start | bytes 393224 | tf_op jit(solution)/shard_map/ppermute | solution.py:32
  11.5 0.4 %collective-permute-done.1.refs_2_ = bf16[4,128,128]{2,1,0:T(8,128)(2,1)S(1)} collective-permute-done((bf16[4,128,128]{2,1,0:T(8,128)(2,1)}, bf16[4,128,128]{2,1,0:T(8,128)(2,1)S(1)}, u32[]{:S(2)}, u32[]{:S(2)}) %collective-permute-start.1) | collective-permute-done | bytes 131104 | tf_op jit(solution)/shard_map/ppermute | solution.py:32
  12.0 0.0 collective-permute-done.refs_1_
  12.0 1.4 %early_products.1 = (f32[3,128,128]{2,1,0:T(8,128)S(1)}, f32[3,128,128]{2,1,0:T(8,128)S(1)}, f32[3,128,128]{2,1,0:T(8,128)S(1)}, f32[3,128,128]{2,1,0:T(8,128)S(1)}) custom-call(s32[1,1,1,4,2,4,12]{6,5,4,3,2,1,0:T(4,128)S(4)} %get-tuple-element.15.lists, bf16[9,128,128]{2,1,0:T(8,128)(2,1)S(1)} %right_panel.1.panel, ...), custom_call_target="tpu_custom_call" | custom-call | flops 12079595520 | tf_op jit(solution)/shard_map/early_products/pallas_call | solution.py:143
  13.4 0.6 %collective-permute-done.3.refs_0_ = bf16[4,128,128]{2,1,0:T(8,128)(2,1)S(1)} collective-permute-done((bf16[4,128,128]{2,1,0:T(8,128)(2,1)S(1)}, bf16[4,128,128]{2,1,0:T(8,128)(2,1)S(1)}, u32[]{:S(2)}, u32[]{:S(2)}) %collective-permute-start.3) | collective-permute-done | bytes 131104 | tf_op jit(solution)/shard_map/ppermute | solution.py:32
  14.1 0.4 %late_products_far.1 = (f32[3,128,128]{2,1,0:T(8,128)S(1)}, f32[3,128,128]{2,1,0:T(8,128)S(1)}) custom-call(s32[1,1,1,4,2,4,12]{6,5,4,3,2,1,0:T(4,128)S(4)} %get-tuple-element.15.lists, bf16[9,128,128]{2,1,0:T(8,128)(2,1)S(1)} %right_panel.1.panel, bf16[4,128,128]{2,1,0:T(8,128)(2,1)S(1)} %collective-permute-done.3.refs_0_, ...), custom_call_target="tpu_custom_call" | custom-call | flops 2013265920 | tf_op jit(solution)/shard_map/late_products_far/pallas_call | solution.py:143
  14.4 0.1 collective-permute-start.5
  14.5 0.4 %late_products_near.1 = (f32[3,128,128]{2,1,0:T(8,128)S(1)}, f32[3,128,128]{2,1,0:T(8,128)S(1)}) custom-call(s32[1,1,1,4,2,4,12]{6,5,4,3,2,1,0:T(4,128)S(4)} %get-tuple-element.15.lists, bf16[9,128,128]{2,1,0:T(8,128)(2,1)S(1)} %right_panel.1.panel, bf16[4,128,128]{2,1,0:T(8,128)(2,1)S(1)} %collective-permute-done.3.refs_0_, ...), custom_call_target="tpu_custom_call" | custom-call | flops 2013265920 | tf_op jit(solution)/shard_map/late_products_near/pallas_call | solution.py:143
  14.9 0.5 %collective-permute-start.4 = (f32[3,128,128]{2,1,0:T(8,128)S(1)}, f32[3,128,128]{2,1,0:T(8,128)S(1)}, u32[]{:S(2)}, u32[]{:S(2)}) collective-permute-start(f32[3,128,128]{2,1,0:T(8,128)S(1)} %get-tuple-element.20), channel_id=1, source_target_pairs={{0,1},{1,0},{2,3},{3,2},{4,5},{5,4},{6,7},{7,6},{8,9},{9,8},{10,11... | collective-permute-start | bytes 589832 | tf_op jit(solution)/shard_map/ppermute | solution.py:18
  15.4 0.5 %collective-permute-done.5 = f32[3,128,128]{2,1,0:T(8,128)S(1)} collective-permute-done((f32[3,128,128]{2,1,0:T(8,128)S(1)}, f32[3,128,128]{2,1,0:T(8,128)S(1)}, u32[]{:S(2)}, u32[]{:S(2)}) %collective-permute-start.5) | collective-permute-done | bytes 196640 | tf_op jit(solution)/shard_map/ppermute | solution.py:18
  16.0 1.6 %collective-permute-start.6 = (f32[3,128,128]{2,1,0:T(8,128)S(1)}, f32[3,128,128]{2,1,0:T(8,128)S(1)}, u32[]{:S(2)}, u32[]{:S(2)}) collective-permute-start(f32[3,128,128]{2,1,0:T(8,128)S(1)} %add.10), channel_id=1, source_target_pairs={{0,2},{1,3},{2,0},{3,1},{4,6},{5,7},{6,4},{7,5},{8,10},{9,11},{10,... | collective-permute-start | bytes 589832 | tf_op jit(solution)/shard_map/ppermute | solution.py:18
  17.5 0.0 collective-permute-done.4
  17.5 5.4 %collective-permute-done.6 = f32[3,128,128]{2,1,0:T(8,128)S(1)} collective-permute-done((f32[3,128,128]{2,1,0:T(8,128)S(1)}, f32[3,128,128]{2,1,0:T(8,128)S(1)}, u32[]{:S(2)}, u32[]{:S(2)}) %collective-permute-start.6) | collective-permute-done | bytes 196640 | tf_op jit(solution)/shard_map/ppermute | solution.py:18
  23.0 0.7 %add_bitcast_fusion = f32[1,1,3,128,128]{4,3,2,1,0:T(8,128)} fusion(f32[3,128,128]{2,1,0:T(8,128)S(1)} %collective-permute-done.6, f32[3,128,128]{2,1,0:T(8,128)S(1)} %get-tuple-element.19, f32[3,128,128]{2,1,0:T(8,128)S(1)} %collective-permute-done.4), kind=kLoop, calls=%fused_computation | loop fusion | flops 98304 | bytes 786432 | tf_op jit(solution)/shard_map/reshape | solution.py:162
  (2 shorter events, 0.1 us)
Async XLA Ops:
  0.0 8.3 %collective-permute-start.2 = (bf16[4,128,128]{2,1,0:T(8,128)(2,1)}, bf16[4,128,128]{2,1,0:T(8,128)(2,1)S(1)}, u32[]{:S(2)}, u32[]{:S(2)}) collective-permute-start(bf16[4,128,128]{2,1,0:T(8,128)(2,1)} %bitcast.3), channel_id=1, source_target_pairs={{0,8},{8,12},{12,4},{4,0},{1,9},{9,13},{13,5},{5,1},{2,10},{10,14}... | collective-permute-start | bytes 393224 | tf_op jit(solution)/shard_map/ppermute | solution.py:32
  4.0 7.9 %collective-permute-start.1 = (bf16[4,128,128]{2,1,0:T(8,128)(2,1)}, bf16[4,128,128]{2,1,0:T(8,128)(2,1)S(1)}, u32[]{:S(2)}, u32[]{:S(2)}) collective-permute-start(bf16[4,128,128]{2,1,0:T(8,128)(2,1)} %bitcast.4), channel_id=1, source_target_pairs={{0,4},{8,0},{12,8},{4,12},{1,5},{9,1},{13,9},{5,13},{2,6},{10,2},{... | collective-permute-start | bytes 393224 | tf_op jit(solution)/shard_map/ppermute | solution.py:32
  4.0 7.9 %collective-permute-start = (bf16[4,128,128]{2,1,0:T(8,128)(2,1)}, bf16[4,128,128]{2,1,0:T(8,128)(2,1)S(1)}, u32[]{:S(2)}, u32[]{:S(2)}) collective-permute-start(bf16[4,128,128]{2,1,0:T(8,128)(2,1)} %bitcast.5), channel_id=1, source_target_pairs={{0,16},{16,0},{1,17},{17,1},{2,18},{18,2},{3,19},{19,3},{4,20},{20... | collective-permute-start | bytes 393224 | tf_op jit(solution)/shard_map/ppermute | solution.py:18
  8.3 5.8 %collective-permute-start.3 = (bf16[4,128,128]{2,1,0:T(8,128)(2,1)S(1)}, bf16[4,128,128]{2,1,0:T(8,128)(2,1)S(1)}, u32[]{:S(2)}, u32[]{:S(2)}) collective-permute-start(bf16[4,128,128]{2,1,0:T(8,128)(2,1)S(1)} %collective-permute-done.2.refs_1_), channel_id=1, source_target_pairs={{0,8},{8,12},{12,4},{4,0},{1,9},{9,13},{13,5},{5,1},{2,10},{10,14}... | collective-permute-start | bytes 393224 | tf_op jit(solution)/shard_map/ppermute | solution.py:32
  14.4 1.5 %collective-permute-start.5 = (f32[3,128,128]{2,1,0:T(8,128)S(1)}, f32[3,128,128]{2,1,0:T(8,128)S(1)}, u32[]{:S(2)}, u32[]{:S(2)}) collective-permute-start(f32[3,128,128]{2,1,0:T(8,128)S(1)} %get-tuple-element.24), channel_id=1, source_target_pairs={{0,1},{1,0},{2,3},{3,2},{4,5},{5,4},{6,7},{7,6},{8,9},{9,8},{10,11... | collective-permute-start | bytes 589832 | tf_op jit(solution)/shard_map/ppermute | solution.py:18
  14.9 2.6 %collective-permute-start.4 = (f32[3,128,128]{2,1,0:T(8,128)S(1)}, f32[3,128,128]{2,1,0:T(8,128)S(1)}, u32[]{:S(2)}, u32[]{:S(2)}) collective-permute-start(f32[3,128,128]{2,1,0:T(8,128)S(1)} %get-tuple-element.20), channel_id=1, source_target_pairs={{0,1},{1,0},{2,3},{3,2},{4,5},{5,4},{6,7},{7,6},{8,9},{9,8},{10,11... | collective-permute-start | bytes 589832 | tf_op jit(solution)/shard_map/ppermute | solution.py:18
  16.0 7.0 %collective-permute-start.6 = (f32[3,128,128]{2,1,0:T(8,128)S(1)}, f32[3,128,128]{2,1,0:T(8,128)S(1)}, u32[]{:S(2)}, u32[]{:S(2)}) collective-permute-start(f32[3,128,128]{2,1,0:T(8,128)S(1)} %add.10), channel_id=1, source_target_pairs={{0,2},{1,3},{2,0},{3,1},{4,6},{5,7},{6,4},{7,5},{8,10},{9,11},{10,... | collective-permute-start | bytes 589832 | tf_op jit(solution)/shard_map/ppermute | solution.py:18

commit v4 on v3

--- a/solution.py
+++ b/solution.py
@@ -11,6 +11,8 @@
 SMEM = pl.BlockSpec(memory_space=pltpu.SMEM)
 ANY = pl.BlockSpec(memory_space=pl.ANY)
 WEIGHT = 20
+TILE = 16
+STEPS = 8
 
 
 def exchange(block, axis, distance):
@@ -96,6 +98,29 @@
             targets[k][i] = total
 
 
+def code_kernel(kept, came, coded):
+    share, width = kept.shape[:2]
+    line = lax.broadcasted_iota(jnp.int32, (TILE, width), 0)
+    powers = jnp.zeros((TILE, width), jnp.float32)
+    for i in range(share):
+        total = kept[i] + came[i]
+        top = jnp.max(jnp.abs(total), axis=0, keepdims=True)
+        power = jnp.floor((15.0 - jnp.log2(jnp.maximum(top, 2.0**-110))) * STEPS)
+        whole = jnp.clip(jnp.round(total * jnp.exp2(power / STEPS)), -32767.0, 32767.0)
+        coded[pl.ds(i * width, width)] = whole.astype(jnp.int32).astype(jnp.int16)
+        powers = jnp.where(line == i, power, powers)
+    coded[pl.ds(share * width, TILE)] = powers.astype(jnp.int32).astype(jnp.int16)
+
+
+def finish_kernel(kept, came, coded, out):
+    share, width = kept.shape[:2]
+    powers = coded[pl.ds(share * width, TILE)].astype(jnp.int32).astype(jnp.float32)
+    scales = jnp.exp2(-powers / STEPS)
+    for i in range(share):
+        whole = coded[pl.ds(i * width, width)].astype(jnp.int32).astype(jnp.float32)
+        out[i] = kept[i] + came[i] + whole * scales[i : i + 1]
+
+
 def body(a_tiles, pair_lists):
     rows, cols, depths = (lax.axis_size(name) for name in ("row", "col", "depth"))
     slots, width = a_tiles.shape[3], a_tiles.shape[4]
@@ -152,14 +177,27 @@
             )(lists, in_vmem(panel), *[in_vmem(lefts[s]) for s in steps], *[in_vmem(s) for s in sums])
         )
 
-    sums = add([s for s in lefts if s != last], [2, 3, 0, 1], [], "early_products")
-    far_kept, far_sent = add([last], [2, 3], sums[:2], "late_products_far")
-    near_kept, near_sent = add([last], [0, 1], sums[2:], "late_products_near")
+    sums = add([s for s in lefts if s != last], [3, 2, 1, 0], [], "early_products")
+    (far_sent,) = add([last], [3], sums[:1], "late_products_first")
+    far_kept, near_sent, near_kept = add([last], [2, 1, 0], sums[1:], "late_products_rest")
     far_came = exchange(far_sent, "depth", 1)
     near_came = exchange(near_sent, "depth", 1)
-    far = far_kept + far_came
-    near = near_kept + near_came
-    return (near + exchange(far, "depth", 2)).reshape(1, 1, share, width, width)
+    coded = pl.pallas_call(
+        code_kernel,
+        out_shape=pltpu.VMEM((share * width + TILE, width), jnp.int16),
+        in_specs=[VMEM] * 2,
+        out_specs=VMEM,
+        name="code",
+    )(in_vmem(far_kept), in_vmem(far_came))
+    coded = exchange(coded, "depth", 2)
+    out = pl.pallas_call(
+        finish_kernel,
+        out_shape=jax.ShapeDtypeStruct((share, width, width), jnp.float32),
+        in_specs=[VMEM] * 3,
+        out_specs=VMEM,
+        name="finish",
+    )(in_vmem(near_kept), in_vmem(near_came), in_vmem(coded))
+    return out.reshape(1, 1, share, width, width)
 
 
 def solution(mesh):

time: 23.9 us -> 21.9 us (0.916)
  waiting for transfers between devices: 8.71 us -> 6.59 us
  Pallas kernels: 3.2 us -> 3.99 us
  other arithmetic: 0.73 us -> 0 us
    ppermute x4, waiting for transfers between devices: 5.94 us -> 3.82 us  [exchange(): return lax.ppermute(block, axis, [(i, i ^ distance) for i in range(size)])]
    pallas_call x0 -> x2, Pallas kernels: none -> 0.79 us  [the longest x1 0.72 us: body(): pl.pallas_call(finish_kernel, out_shape=jax.ShapeDtypeStruct((share, widt...]
    reshape x1 -> x0, other arithmetic: 0.71 us -> none  [body(): return (near + exchange(far, 'depth', 2)).reshape(1, 1, share, width, width)]
  transfers between devices with their start and end apart: 7 -> 7, of which waited for: 5 -> 5; matrix products, arithmetic and copies ran while one was open for 0% -> 0% of each run, Pallas kernels for 12% -> 14%
where the time goes in v4:
time: 21.9 us; the launch traced here: 21.6 us
  starting transfers between devices  11 us (50%)
  waiting for transfers between devices  6.59 us (30%)
  Pallas kernels  3.99 us (18%)
    ppermute x3, starting transfers between devices, turn(): lax.ppermute(block, axis, [(ring[i], ring[(i + step) % size]) for i in ra...  7.31 us
    ppermute x4, waiting for transfers between devices, exchange(): return lax.ppermute(block, axis, [(i, i ^ distance) for i in range(size)])  3.82 us
    ppermute x4, starting transfers between devices, exchange(): return lax.ppermute(block, axis, [(i, i ^ distance) for i in range(size)])  3.67 us
    ppermute x3, waiting for transfers between devices, turn(): lax.ppermute(block, axis, [(ring[i], ring[(i + step) % size]) for i in ra...  2.77 us
    pallas_call x3, Pallas kernels, add(): pl.pallas_call(functools.partial(add_kernel, steps, groups, bool(sums)),...  2.22 us
    pallas_call x1, Pallas kernels, body(): pl.pallas_call(stage_kernel, out_shape=(pltpu.SMEM(pair_lists.shape, jnp....  0.95 us
    pallas_call x1, Pallas kernels, body(): pl.pallas_call(finish_kernel, out_shape=jax.ShapeDtypeStruct((share, widt...  0.72 us
  transfers between devices with their start and end apart: 7, of which 5 were waited for; matrix products, arithmetic and copies ran while one was open for 0% of the time, Pallas kernels for 14%

profile of v4, /device:TPU:0, one launch (start us, length us, event | category | flops | bytes accessed | tf_op | source)
XLA Modules:
  0.0 21.6 jit_solution(6946648859532003066)
XLA Ops:
  0.0 4.0 %collective-permute-start.2 = (bf16[4,128,128]{2,1,0:T(8,128)(2,1)}, bf16[4,128,128]{2,1,0:T(8,128)(2,1)S(1)}, u32[]{:S(2)}, u32[]{:S(2)}) collective-permute-start(bf16[4,128,128]{2,1,0:T(8,128)(2,1)} %bitcast.2), channel_id=1, source_target_pairs={{0,8},{8,12},{12,4},{4,0},{1,9},{9,13},{13,5},{5,1},{2,10},{10,14}... | collective-permute-start | bytes 393224 | tf_op jit(solution)/shard_map/ppermute | solution.py:34
  4.0 0.0 collective-permute-start.1
  4.0 1.5 %collective-permute-start = (bf16[4,128,128]{2,1,0:T(8,128)(2,1)}, bf16[4,128,128]{2,1,0:T(8,128)(2,1)S(1)}, u32[]{:S(2)}, u32[]{:S(2)}) collective-permute-start(bf16[4,128,128]{2,1,0:T(8,128)(2,1)} %bitcast.4), channel_id=1, source_target_pairs={{0,16},{16,0},{1,17},{17,1},{2,18},{18,2},{3,19},{19,3},{4,20},{20... | collective-permute-start | bytes 393224 | tf_op jit(solution)/shard_map/ppermute | solution.py:20
  5.6 1.0 %stage.1 = (s32[1,1,1,4,2,4,12]{6,5,4,3,2,1,0:T(4,128)S(4)}, bf16[4,128,128]{2,1,0:T(8,128)(2,1)S(1)}) custom-call(bf16[4,128,128]{2,1,0:T(8,128)(2,1)} %bitcast.5, s32[1,1,1,4,2,4,12]{6,5,4,3,2,1,0:T(4,128)} %lists.1), custom_call_target="tpu_custom_call" | custom-call | tf_op jit(solution)/shard_map/stage/pallas_call | solution.py:131
  6.5 1.7 %collective-permute-done.2.refs_1_ = bf16[4,128,128]{2,1,0:T(8,128)(2,1)S(1)} collective-permute-done((bf16[4,128,128]{2,1,0:T(8,128)(2,1)}, bf16[4,128,128]{2,1,0:T(8,128)(2,1)S(1)}, u32[]{:S(2)}, u32[]{:S(2)}) %collective-permute-start.2) | collective-permute-done | bytes 131104 | tf_op jit(solution)/shard_map/ppermute | solution.py:34
  8.3 3.3 %collective-permute-start.3 = (bf16[4,128,128]{2,1,0:T(8,128)(2,1)S(1)}, bf16[4,128,128]{2,1,0:T(8,128)(2,1)S(1)}, u32[]{:S(2)}, u32[]{:S(2)}) collective-permute-start(bf16[4,128,128]{2,1,0:T(8,128)(2,1)S(1)} %collective-permute-done.2.refs_1_), channel_id=1, source_target_pairs={{0,8},{8,12},{12,4},{4,0},{1,9},{9,13},{13,5},{5,1},{2,10},{10,14}... | collective-permute-start | bytes 393224 | tf_op jit(solution)/shard_map/ppermute | solution.py:34
  11.5 0.4 %collective-permute-done.1.refs_2_ = bf16[4,128,128]{2,1,0:T(8,128)(2,1)S(1)} collective-permute-done((bf16[4,128,128]{2,1,0:T(8,128)(2,1)}, bf16[4,128,128]{2,1,0:T(8,128)(2,1)S(1)}, u32[]{:S(2)}, u32[]{:S(2)}) %collective-permute-start.1) | collective-permute-done | bytes 131104 | tf_op jit(solution)/shard_map/ppermute | solution.py:34
  12.0 0.0 collective-permute-done.refs_1_
  12.0 1.4 %early_products.1 = (f32[3,128,128]{2,1,0:T(8,128)S(1)}, f32[3,128,128]{2,1,0:T(8,128)S(1)}, f32[3,128,128]{2,1,0:T(8,128)S(1)}, f32[3,128,128]{2,1,0:T(8,128)S(1)}) custom-call(s32[1,1,1,4,2,4,12]{6,5,4,3,2,1,0:T(4,128)S(4)} %get-tuple-element.14.lists, bf16[9,128,128]{2,1,0:T(8,128)(2,1)S(1)} %right_panel.1.panel, ...), custom_call_target="tpu_custom_call" | custom-call | flops 12079595520 | tf_op jit(solution)/shard_map/early_products/pallas_call | solution.py:168
  13.4 0.6 %collective-permute-done.3.refs_0_ = bf16[4,128,128]{2,1,0:T(8,128)(2,1)S(1)} collective-permute-done((bf16[4,128,128]{2,1,0:T(8,128)(2,1)S(1)}, bf16[4,128,128]{2,1,0:T(8,128)(2,1)S(1)}, u32[]{:S(2)}, u32[]{:S(2)}) %collective-permute-start.3) | collective-permute-done | bytes 131104 | tf_op jit(solution)/shard_map/ppermute | solution.py:34
  14.1 0.3 %late_products_first.1 = f32[3,128,128]{2,1,0:T(8,128)S(1)} custom-call(s32[1,1,1,4,2,4,12]{6,5,4,3,2,1,0:T(4,128)S(4)} %get-tuple-element.14.lists, bf16[9,128,128]{2,1,0:T(8,128)(2,1)S(1)} %right_panel.1.panel, bf16[4,128,128]{2,1,0:T(8,128)(2,1)S(1)} %collective-permute-done.3.refs_0_, f32[3,128,128]{2,1,0:T(8,128)S(1)} %get-tuple-element.22.refs_1_), custom_call_target="tpu_custom_call" | custom-call | flops 1006632960 | tf_op jit(solution)/shard_map/late_products_first/pallas_call | solution.py:168
  14.3 0.1 collective-permute-start.5
  14.4 0.5 %late_products_rest.1 = (f32[3,128,128]{2,1,0:T(8,128)S(1)}, f32[3,128,128]{2,1,0:T(8,128)S(1)}, f32[3,128,128]{2,1,0:T(8,128)S(1)}) custom-call(s32[1,1,1,4,2,4,12]{6,5,4,3,2,1,0:T(4,128)S(4)} %get-tuple-element.14.lists, bf16[9,128,128]{2,1,0:T(8,128)(2,1)S(1)} %right_panel.1.panel, bf16[4,128,128]{2,1,0:T(8,128)(2,1)S(1)} %collective-permute-done.3.refs_0_, ...), custom_call_target="tpu_custom_call" | custom-call | flops 3019898880 | tf_op jit(solution)/shard_map/late_products_rest/pallas_call | solution.py:168
  14.9 0.5 %collective-permute-start.4 = (f32[3,128,128]{2,1,0:T(8,128)S(1)}, f32[3,128,128]{2,1,0:T(8,128)S(1)}, u32[]{:S(2)}, u32[]{:S(2)}) collective-permute-start(f32[3,128,128]{2,1,0:T(8,128)S(1)} %get-tuple-element.20), channel_id=1, source_target_pairs={{0,1},{1,0},{2,3},{3,2},{4,5},{5,4},{6,7},{7,6},{8,9},{9,8},{10,11... | collective-permute-start | bytes 589832 | tf_op jit(solution)/shard_map/ppermute | solution.py:20
  15.4 0.4 %collective-permute-done.5.came = f32[3,128,128]{2,1,0:T(8,128)S(1)} collective-permute-done((f32[3,128,128]{2,1,0:T(8,128)S(1)}, f32[3,128,128]{2,1,0:T(8,128)S(1)}, u32[]{:S(2)}, u32[]{:S(2)}) %collective-permute-start.5) | collective-permute-done | bytes 196640 | tf_op jit(solution)/shard_map/ppermute | solution.py:20
  15.8 0.1 code.1
  15.9 1.6 %collective-permute-start.6 = (s16[400,128]{1,0:T(8,128)(2,1)S(1)}, s16[400,128]{1,0:T(8,128)(2,1)S(1)}, u32[]{:S(2)}, u32[]{:S(2)}) collective-permute-start(s16[400,128]{1,0:T(8,128)(2,1)S(1)} %code.1), channel_id=1, source_target_pairs={{0,2},{1,3},{2,0},{3,1},{4,6},{5,7},{6,4},{7,5},{8,10},{9,11},{10,... | collective-permute-start | bytes 307208 | tf_op jit(solution)/shard_map/ppermute | solution.py:20
  17.5 0.0 collective-permute-done.4.came
  17.5 3.4 %collective-permute-done.6.coded = s16[400,128]{1,0:T(8,128)(2,1)S(1)} collective-permute-done((s16[400,128]{1,0:T(8,128)(2,1)S(1)}, s16[400,128]{1,0:T(8,128)(2,1)S(1)}, u32[]{:S(2)}, u32[]{:S(2)}) %collective-permute-start.6) | collective-permute-done | bytes 102432 | tf_op jit(solution)/shard_map/ppermute | solution.py:20
  20.9 0.7 %finish.1 = f32[3,128,128]{2,1,0:T(8,128)} custom-call(f32[3,128,128]{2,1,0:T(8,128)S(1)} %get-tuple-element.19.kept, f32[3,128,128]{2,1,0:T(8,128)S(1)} %collective-permute-done.4.came, s16[400,128]{1,0:T(8,128)(2,1)S(1)} %collective-permute-done.6.coded), custom_call_target="tpu_custom_call" | custom-call | tf_op jit(solution)/shard_map/finish/pallas_call | solution.py:193
  (1 shorter events, 0.0 us)
Async XLA Ops:
  0.0 8.3 %collective-permute-start.2 = (bf16[4,128,128]{2,1,0:T(8,128)(2,1)}, bf16[4,128,128]{2,1,0:T(8,128)(2,1)S(1)}, u32[]{:S(2)}, u32[]{:S(2)}) collective-permute-start(bf16[4,128,128]{2,1,0:T(8,128)(2,1)} %bitcast.2), channel_id=1, source_target_pairs={{0,8},{8,12},{12,4},{4,0},{1,9},{9,13},{13,5},{5,1},{2,10},{10,14}... | collective-permute-start | bytes 393224 | tf_op jit(solution)/shard_map/ppermute | solution.py:34
  4.0 7.9 %collective-permute-start.1 = (bf16[4,128,128]{2,1,0:T(8,128)(2,1)}, bf16[4,128,128]{2,1,0:T(8,128)(2,1)S(1)}, u32[]{:S(2)}, u32[]{:S(2)}) collective-permute-start(bf16[4,128,128]{2,1,0:T(8,128)(2,1)} %bitcast.3), channel_id=1, source_target_pairs={{0,4},{8,0},{12,8},{4,12},{1,5},{9,1},{13,9},{5,13},{2,6},{10,2},{... | collective-permute-start | bytes 393224 | tf_op jit(solution)/shard_map/ppermute | solution.py:34
  4.0 7.9 %collective-permute-start = (bf16[4,128,128]{2,1,0:T(8,128)(2,1)}, bf16[4,128,128]{2,1,0:T(8,128)(2,1)S(1)}, u32[]{:S(2)}, u32[]{:S(2)}) collective-permute-start(bf16[4,128,128]{2,1,0:T(8,128)(2,1)} %bitcast.4), channel_id=1, source_target_pairs={{0,16},{16,0},{1,17},{17,1},{2,18},{18,2},{3,19},{19,3},{4,20},{20... | collective-permute-start | bytes 393224 | tf_op jit(solution)/shard_map/ppermute | solution.py:20
  8.3 5.8 %collective-permute-start.3 = (bf16[4,128,128]{2,1,0:T(8,128)(2,1)S(1)}, bf16[4,128,128]{2,1,0:T(8,128)(2,1)S(1)}, u32[]{:S(2)}, u32[]{:S(2)}) collective-permute-start(bf16[4,128,128]{2,1,0:T(8,128)(2,1)S(1)} %collective-permute-done.2.refs_1_), channel_id=1, source_target_pairs={{0,8},{8,12},{12,4},{4,0},{1,9},{9,13},{13,5},{5,1},{2,10},{10,14}... | collective-permute-start | bytes 393224 | tf_op jit(solution)/shard_map/ppermute | solution.py:34
  14.3 1.5 %collective-permute-start.5 = (f32[3,128,128]{2,1,0:T(8,128)S(1)}, f32[3,128,128]{2,1,0:T(8,128)S(1)}, u32[]{:S(2)}, u32[]{:S(2)}) collective-permute-start(f32[3,128,128]{2,1,0:T(8,128)S(1)} %late_products_first.1), channel_id=1, source_target_pairs={{0,1},{1,0},{2,3},{3,2},{4,5},{5,4},{6,7},{7,6},{8,9},{9,8},{10,11... | collective-permute-start | bytes 589832 | tf_op jit(solution)/shard_map/ppermute | solution.py:20
  14.9 2.5 %collective-permute-start.4 = (f32[3,128,128]{2,1,0:T(8,128)S(1)}, f32[3,128,128]{2,1,0:T(8,128)S(1)}, u32[]{:S(2)}, u32[]{:S(2)}) collective-permute-start(f32[3,128,128]{2,1,0:T(8,128)S(1)} %get-tuple-element.20), channel_id=1, source_target_pairs={{0,1},{1,0},{2,3},{3,2},{4,5},{5,4},{6,7},{7,6},{8,9},{9,8},{10,11... | collective-permute-start | bytes 589832 | tf_op jit(solution)/shard_map/ppermute | solution.py:20
  15.9 5.0 %collective-permute-start.6 = (s16[400,128]{1,0:T(8,128)(2,1)S(1)}, s16[400,128]{1,0:T(8,128)(2,1)S(1)}, u32[]{:S(2)}, u32[]{:S(2)}) collective-permute-start(s16[400,128]{1,0:T(8,128)(2,1)S(1)} %code.1), channel_id=1, source_target_pairs={{0,2},{1,3},{2,0},{3,1},{4,6},{5,7},{6,4},{7,5},{8,10},{9,11},{10,... | collective-permute-start | bytes 307208 | tf_op jit(solution)/shard_map/ppermute | solution.py:20

commit v5 on v4

--- a/solution.py
+++ b/solution.py
@@ -58,13 +58,12 @@
     panel[len(sources) * slots] = jnp.zeros(panel.shape[1:], panel.dtype)
 
 
-def add_kernel(steps, groups, started, lists, panel, *refs):
+def add_kernel(steps, groups, share, started, coded, lists, panel, *refs):
     lefts, refs = refs[: len(steps)], refs[len(steps) :]
     sources, targets = (refs[: len(groups)], refs[len(groups) :]) if started else (None, refs)
     cols, pairs = lists.shape[3], lists.shape[5]
     slots = lefts[0].shape[0]
     zero_slot = panel.shape[0] - 1
-    share = targets[0].shape[0]
     col, layer = lax.axis_index("col"), lax.axis_index("depth")
     width = 2 if pairs % 2 == 0 else 1
 
@@ -89,27 +88,46 @@
         return total
 
     for k, group in enumerate(groups):
+        totals = []
         for i in range(share):
             out = (layer ^ group) * share + i
             total = sources[k][i] if started else None
             for step, left in zip(steps, lefts):
                 term = products(step, left, out)
                 total = term if total is None else total + term
+            totals.append(total)
+        if coded:
+            encode(totals, targets[k])
+            continue
+        for i, total in enumerate(totals):
             targets[k][i] = total
 
 
-def code_kernel(kept, came, coded):
-    share, width = kept.shape[:2]
+def encode(blocks, coded):
+    width = blocks[0].shape[0]
     line = lax.broadcasted_iota(jnp.int32, (TILE, width), 0)
     powers = jnp.zeros((TILE, width), jnp.float32)
-    for i in range(share):
-        total = kept[i] + came[i]
+    for i, total in enumerate(blocks):
         top = jnp.max(jnp.abs(total), axis=0, keepdims=True)
         power = jnp.floor((15.0 - jnp.log2(jnp.maximum(top, 2.0**-110))) * STEPS)
         whole = jnp.clip(jnp.round(total * jnp.exp2(power / STEPS)), -32767.0, 32767.0)
         coded[pl.ds(i * width, width)] = whole.astype(jnp.int32).astype(jnp.int16)
         powers = jnp.where(line == i, power, powers)
-    coded[pl.ds(share * width, TILE)] = powers.astype(jnp.int32).astype(jnp.int16)
+    coded[pl.ds(len(blocks) * width, TILE)] = powers.astype(jnp.int32).astype(jnp.int16)
+
+
+def code_kernel(kept, came, coded):
+    encode([kept[i] + block for i, block in enumerate(decode(came))], coded)
+
+
+def decode(coded):
+    width = coded.shape[1]
+    count = coded.shape[0] // width
+    powers = coded[pl.ds(count * width, TILE)].astype(jnp.int32).astype(jnp.float32)
+    scales = jnp.exp2(-powers / STEPS)
+    for i in range(count):
+        whole = coded[pl.ds(i * width, width)].astype(jnp.int32).astype(jnp.float32)
+        yield whole * scales[i : i + 1]
 
 
 def finish_kernel(kept, came, coded, out):
@@ -161,13 +179,14 @@
     )(*[in_vmem(rights[i]) for i in range(rows)], in_vmem(lefts[min(lefts)]))
 
     block = pltpu.VMEM((share, width, width), jnp.float32)
-
-    def add(steps, groups, sums, name):
+    code = pltpu.VMEM((share * width + TILE, width), jnp.int16)
+
+    def add(steps, groups, sums, name, coded=False):
         flops = 2 * width**3 * pairs * share * len(groups) * len(steps)
         return list(
             pl.pallas_call(
-                functools.partial(add_kernel, steps, groups, bool(sums)),
-                out_shape=[block] * len(groups),
+                functools.partial(add_kernel, steps, groups, share, bool(sums), coded),
+                out_shape=[code if coded else block] * len(groups),
                 in_specs=[SMEM] + [VMEM] * (1 + len(steps) + len(sums)),
                 out_specs=[VMEM] * len(groups),
                 name=name,
@@ -177,9 +196,9 @@
             )(lists, in_vmem(panel), *[in_vmem(lefts[s]) for s in steps], *[in_vmem(s) for s in sums])
         )
 
-    sums = add([s for s in lefts if s != last], [3, 2, 1, 0], [], "early_products")
-    (far_sent,) = add([last], [3], sums[:1], "late_products_first")
-    far_kept, near_sent, near_kept = add([last], [2, 1, 0], sums[1:], "late_products_rest")
+    sums = add([s for s in lefts if s != last], [2, 3, 1, 0], [], "early_products")
+    (far_sent,) = add([last], [2], sums[:1], "late_products_first", True)
+    far_kept, near_sent, near_kept = add([last], [3, 1, 0], sums[1:], "late_products_rest")
     far_came = exchange(far_sent, "depth", 1)
     near_came = exchange(near_sent, "depth", 1)
     coded = pl.pallas_call(
@@ -189,7 +208,7 @@
         out_specs=VMEM,
         name="code",
     )(in_vmem(far_kept), in_vmem(far_came))
-    coded = exchange(coded, "depth", 2)
+    coded = exchange(coded, "depth", 3)
     out = pl.pallas_call(
         finish_kernel,
         out_shape=jax.ShapeDtypeStruct((share, width, width), jnp.float32),

time: 21.9 us -> 21.7 us (level)
  starting transfers between devices: 11 us -> 10.7 us
    ppermute x4, starting transfers between devices: 3.67 us -> 3.43 us  [exchange(): return lax.ppermute(block, axis, [(i, i ^ distance) for i in range(size)])]
where the time goes in v5:
time: 21.7 us; the launch traced here: 21.5 us
  starting transfers between devices  10.7 us (49%)
  waiting for transfers between devices  6.62 us (31%)
  Pallas kernels  4.05 us (19%)
    ppermute x3, starting transfers between devices, turn(): lax.ppermute(block, axis, [(ring[i], ring[(i + step) % size]) for i in ra...  7.31 us
    ppermute x4, waiting for transfers between devices, exchange(): return lax.ppermute(block, axis, [(i, i ^ distance) for i in range(size)])  3.85 us
    ppermute x4, starting transfers between devices, exchange(): return lax.ppermute(block, axis, [(i, i ^ distance) for i in range(size)])  3.43 us
    ppermute x3, waiting for transfers between devices, turn(): lax.ppermute(block, axis, [(ring[i], ring[(i + step) % size]) for i in ra...  2.77 us
    pallas_call x3, Pallas kernels, add(): pl.pallas_call(functools.partial(add_kernel, steps, groups, share, bool(s...  2.26 us
    pallas_call x1, Pallas kernels, body(): pl.pallas_call(stage_kernel, out_shape=(pltpu.SMEM(pair_lists.shape, jnp....  0.95 us
    pallas_call x1, Pallas kernels, body(): pl.pallas_call(finish_kernel, out_shape=jax.ShapeDtypeStruct((share, widt...  0.72 us
  transfers between devices with their start and end apart: 7, of which 5 were waited for; matrix products, arithmetic and copies ran while one was open for 0% of the time, Pallas kernels for 14%

profile of v5, /device:TPU:0, one launch (start us, length us, event | category | flops | bytes accessed | tf_op | source)
XLA Modules:
  0.0 21.5 jit_solution(6044404403093354253)
XLA Ops:
  0.0 4.0 %collective-permute-start.2 = (bf16[4,128,128]{2,1,0:T(8,128)(2,1)}, bf16[4,128,128]{2,1,0:T(8,128)(2,1)S(1)}, u32[]{:S(2)}, u32[]{:S(2)}) collective-permute-start(bf16[4,128,128]{2,1,0:T(8,128)(2,1)} %bitcast.2), channel_id=1, source_target_pairs={{0,8},{8,12},{12,4},{4,0},{1,9},{9,13},{13,5},{5,1},{2,10},{10,14}... | collective-permute-start | bytes 393224 | tf_op jit(solution)/shard_map/ppermute | solution.py:34
  4.0 0.0 collective-permute-start.1
  4.0 1.5 %collective-permute-start = (bf16[4,128,128]{2,1,0:T(8,128)(2,1)}, bf16[4,128,128]{2,1,0:T(8,128)(2,1)S(1)}, u32[]{:S(2)}, u32[]{:S(2)}) collective-permute-start(bf16[4,128,128]{2,1,0:T(8,128)(2,1)} %bitcast.4), channel_id=1, source_target_pairs={{0,16},{16,0},{1,17},{17,1},{2,18},{18,2},{3,19},{19,3},{4,20},{20... | collective-permute-start | bytes 393224 | tf_op jit(solution)/shard_map/ppermute | solution.py:20
  5.6 1.0 %stage.1 = (s32[1,1,1,4,2,4,12]{6,5,4,3,2,1,0:T(4,128)S(4)}, bf16[4,128,128]{2,1,0:T(8,128)(2,1)S(1)}) custom-call(bf16[4,128,128]{2,1,0:T(8,128)(2,1)} %bitcast.5, s32[1,1,1,4,2,4,12]{6,5,4,3,2,1,0:T(4,128)} %lists.1), custom_call_target="tpu_custom_call" | custom-call | tf_op jit(solution)/shard_map/stage/pallas_call | solution.py:149
  6.5 1.7 %collective-permute-done.2.refs_1_ = bf16[4,128,128]{2,1,0:T(8,128)(2,1)S(1)} collective-permute-done((bf16[4,128,128]{2,1,0:T(8,128)(2,1)}, bf16[4,128,128]{2,1,0:T(8,128)(2,1)S(1)}, u32[]{:S(2)}, u32[]{:S(2)}) %collective-permute-start.2) | collective-permute-done | bytes 131104 | tf_op jit(solution)/shard_map/ppermute | solution.py:34
  8.3 3.3 %collective-permute-start.3 = (bf16[4,128,128]{2,1,0:T(8,128)(2,1)S(1)}, bf16[4,128,128]{2,1,0:T(8,128)(2,1)S(1)}, u32[]{:S(2)}, u32[]{:S(2)}) collective-permute-start(bf16[4,128,128]{2,1,0:T(8,128)(2,1)S(1)} %collective-permute-done.2.refs_1_), channel_id=1, source_target_pairs={{0,8},{8,12},{12,4},{4,0},{1,9},{9,13},{13,5},{5,1},{2,10},{10,14}... | collective-permute-start | bytes 393224 | tf_op jit(solution)/shard_map/ppermute | solution.py:34
  11.5 0.4 %collective-permute-done.1.refs_2_ = bf16[4,128,128]{2,1,0:T(8,128)(2,1)S(1)} collective-permute-done((bf16[4,128,128]{2,1,0:T(8,128)(2,1)}, bf16[4,128,128]{2,1,0:T(8,128)(2,1)S(1)}, u32[]{:S(2)}, u32[]{:S(2)}) %collective-permute-start.1) | collective-permute-done | bytes 131104 | tf_op jit(solution)/shard_map/ppermute | solution.py:34
  12.0 0.0 collective-permute-done.refs_1_
  12.0 1.4 %early_products.1 = (f32[3,128,128]{2,1,0:T(8,128)S(1)}, f32[3,128,128]{2,1,0:T(8,128)S(1)}, f32[3,128,128]{2,1,0:T(8,128)S(1)}, f32[3,128,128]{2,1,0:T(8,128)S(1)}) custom-call(s32[1,1,1,4,2,4,12]{6,5,4,3,2,1,0:T(4,128)S(4)} %get-tuple-element.14.lists, bf16[9,128,128]{2,1,0:T(8,128)(2,1)S(1)} %right_panel.1.panel, ...), custom_call_target="tpu_custom_call" | custom-call | flops 12079595520 | tf_op jit(solution)/shard_map/early_products/pallas_call | solution.py:187
  13.4 0.6 %collective-permute-done.3.refs_0_ = bf16[4,128,128]{2,1,0:T(8,128)(2,1)S(1)} collective-permute-done((bf16[4,128,128]{2,1,0:T(8,128)(2,1)S(1)}, bf16[4,128,128]{2,1,0:T(8,128)(2,1)S(1)}, u32[]{:S(2)}, u32[]{:S(2)}) %collective-permute-start.3) | collective-permute-done | bytes 131104 | tf_op jit(solution)/shard_map/ppermute | solution.py:34
  14.1 0.3 %late_products_first.1 = s16[400,128]{1,0:T(8,128)(2,1)S(1)} custom-call(s32[1,1,1,4,2,4,12]{6,5,4,3,2,1,0:T(4,128)S(4)} %get-tuple-element.14.lists, bf16[9,128,128]{2,1,0:T(8,128)(2,1)S(1)} %right_panel.1.panel, bf16[4,128,128]{2,1,0:T(8,128)(2,1)S(1)} %collective-permute-done.3.refs_0_, f32[3,128,128]{2,1,0:T(8,128)S(1)} %get-tuple-element.22.refs_1_), custom_call_target="tpu_custom_call" | custom-call | flops 1006632960 | tf_op jit(solution)/shard_map/late_products_first/pallas_call | solution.py:187
  14.4 0.1 collective-permute-start.5
  14.4 0.5 %late_products_rest.1 = (f32[3,128,128]{2,1,0:T(8,128)S(1)}, f32[3,128,128]{2,1,0:T(8,128)S(1)}, f32[3,128,128]{2,1,0:T(8,128)S(1)}) custom-call(s32[1,1,1,4,2,4,12]{6,5,4,3,2,1,0:T(4,128)S(4)} %get-tuple-element.14.lists, bf16[9,128,128]{2,1,0:T(8,128)(2,1)S(1)} %right_panel.1.panel, bf16[4,128,128]{2,1,0:T(8,128)(2,1)S(1)} %collective-permute-done.3.refs_0_, ...), custom_call_target="tpu_custom_call" | custom-call | flops 3019898880 | tf_op jit(solution)/shard_map/late_products_rest/pallas_call | solution.py:187
  15.0 0.5 %collective-permute-start.4 = (f32[3,128,128]{2,1,0:T(8,128)S(1)}, f32[3,128,128]{2,1,0:T(8,128)S(1)}, u32[]{:S(2)}, u32[]{:S(2)}) collective-permute-start(f32[3,128,128]{2,1,0:T(8,128)S(1)} %get-tuple-element.20), channel_id=1, source_target_pairs={{0,1},{1,0},{2,3},{3,2},{4,5},{5,4},{6,7},{7,6},{8,9},{9,8},{10,11... | collective-permute-start | bytes 589832 | tf_op jit(solution)/shard_map/ppermute | solution.py:20
  15.5 0.3 %collective-permute-done.5.came = s16[400,128]{1,0:T(8,128)(2,1)S(1)} collective-permute-done((s16[400,128]{1,0:T(8,128)(2,1)S(1)}, s16[400,128]{1,0:T(8,128)(2,1)S(1)}, u32[]{:S(2)}, u32[]{:S(2)}) %collective-permute-start.5) | collective-permute-done | bytes 102432 | tf_op jit(solution)/shard_map/ppermute | solution.py:20
  15.7 0.1 code.1
  15.8 1.3 %collective-permute-start.6 = (s16[400,128]{1,0:T(8,128)(2,1)S(1)}, s16[400,128]{1,0:T(8,128)(2,1)S(1)}, u32[]{:S(2)}, u32[]{:S(2)}) collective-permute-start(s16[400,128]{1,0:T(8,128)(2,1)S(1)} %code.1), channel_id=1, source_target_pairs={{0,3},{1,2},{2,1},{3,0},{4,7},{5,6},{6,5},{7,4},{8,11},{9,10},{10,... | collective-permute-start | bytes 307208 | tf_op jit(solution)/shard_map/ppermute | solution.py:20
  17.1 0.0 collective-permute-done.4.came
  17.2 3.6 %collective-permute-done.6.coded = s16[400,128]{1,0:T(8,128)(2,1)S(1)} collective-permute-done((s16[400,128]{1,0:T(8,128)(2,1)S(1)}, s16[400,128]{1,0:T(8,128)(2,1)S(1)}, u32[]{:S(2)}, u32[]{:S(2)}) %collective-permute-start.6) | collective-permute-done | bytes 102432 | tf_op jit(solution)/shard_map/ppermute | solution.py:20
  20.7 0.7 %finish.1 = f32[3,128,128]{2,1,0:T(8,128)} custom-call(f32[3,128,128]{2,1,0:T(8,128)S(1)} %get-tuple-element.19.kept, f32[3,128,128]{2,1,0:T(8,128)S(1)} %collective-permute-done.4.came, s16[400,128]{1,0:T(8,128)(2,1)S(1)} %collective-permute-done.6.coded), custom_call_target="tpu_custom_call" | custom-call | tf_op jit(solution)/shard_map/finish/pallas_call | solution.py:212
  (1 shorter events, 0.0 us)
Async XLA Ops:
  0.0 8.3 %collective-permute-start.2 = (bf16[4,128,128]{2,1,0:T(8,128)(2,1)}, bf16[4,128,128]{2,1,0:T(8,128)(2,1)S(1)}, u32[]{:S(2)}, u32[]{:S(2)}) collective-permute-start(bf16[4,128,128]{2,1,0:T(8,128)(2,1)} %bitcast.2), channel_id=1, source_target_pairs={{0,8},{8,12},{12,4},{4,0},{1,9},{9,13},{13,5},{5,1},{2,10},{10,14}... | collective-permute-start | bytes 393224 | tf_op jit(solution)/shard_map/ppermute | solution.py:34
  4.0 7.9 %collective-permute-start.1 = (bf16[4,128,128]{2,1,0:T(8,128)(2,1)}, bf16[4,128,128]{2,1,0:T(8,128)(2,1)S(1)}, u32[]{:S(2)}, u32[]{:S(2)}) collective-permute-start(bf16[4,128,128]{2,1,0:T(8,128)(2,1)} %bitcast.3), channel_id=1, source_target_pairs={{0,4},{8,0},{12,8},{4,12},{1,5},{9,1},{13,9},{5,13},{2,6},{10,2},{... | collective-permute-start | bytes 393224 | tf_op jit(solution)/shard_map/ppermute | solution.py:34
  4.0 7.9 %collective-permute-start = (bf16[4,128,128]{2,1,0:T(8,128)(2,1)}, bf16[4,128,128]{2,1,0:T(8,128)(2,1)S(1)}, u32[]{:S(2)}, u32[]{:S(2)}) collective-permute-start(bf16[4,128,128]{2,1,0:T(8,128)(2,1)} %bitcast.4), channel_id=1, source_target_pairs={{0,16},{16,0},{1,17},{17,1},{2,18},{18,2},{3,19},{19,3},{4,20},{20... | collective-permute-start | bytes 393224 | tf_op jit(solution)/shard_map/ppermute | solution.py:20
  8.3 5.8 %collective-permute-start.3 = (bf16[4,128,128]{2,1,0:T(8,128)(2,1)S(1)}, bf16[4,128,128]{2,1,0:T(8,128)(2,1)S(1)}, u32[]{:S(2)}, u32[]{:S(2)}) collective-permute-start(bf16[4,128,128]{2,1,0:T(8,128)(2,1)S(1)} %collective-permute-done.2.refs_1_), channel_id=1, source_target_pairs={{0,8},{8,12},{12,4},{4,0},{1,9},{9,13},{13,5},{5,1},{2,10},{10,14}... | collective-permute-start | bytes 393224 | tf_op jit(solution)/shard_map/ppermute | solution.py:34
  14.4 1.4 %collective-permute-start.5 = (s16[400,128]{1,0:T(8,128)(2,1)S(1)}, s16[400,128]{1,0:T(8,128)(2,1)S(1)}, u32[]{:S(2)}, u32[]{:S(2)}) collective-permute-start(s16[400,128]{1,0:T(8,128)(2,1)S(1)} %late_products_first.1), channel_id=1, source_target_pairs={{0,1},{1,0},{2,3},{3,2},{4,5},{5,4},{6,7},{7,6},{8,9},{9,8},{10,11... | collective-permute-start | bytes 307208 | tf_op jit(solution)/shard_map/ppermute | solution.py:20
  15.0 2.2 %collective-permute-start.4 = (f32[3,128,128]{2,1,0:T(8,128)S(1)}, f32[3,128,128]{2,1,0:T(8,128)S(1)}, u32[]{:S(2)}, u32[]{:S(2)}) collective-permute-start(f32[3,128,128]{2,1,0:T(8,128)S(1)} %get-tuple-element.20), channel_id=1, source_target_pairs={{0,1},{1,0},{2,3},{3,2},{4,5},{5,4},{6,7},{7,6},{8,9},{9,8},{10,11... | collective-permute-start | bytes 589832 | tf_op jit(solution)/shard_map/ppermute | solution.py:20
  15.8 4.9 %collective-permute-start.6 = (s16[400,128]{1,0:T(8,128)(2,1)S(1)}, s16[400,128]{1,0:T(8,128)(2,1)S(1)}, u32[]{:S(2)}, u32[]{:S(2)}) collective-permute-start(s16[400,128]{1,0:T(8,128)(2,1)S(1)} %code.1), channel_id=1, source_target_pairs={{0,3},{1,2},{2,1},{3,0},{4,7},{5,6},{6,5},{7,4},{8,11},{9,10},{10,... | collective-permute-start | bytes 307208 | tf_op jit(solution)/shard_map/ppermute | solution.py:20

commit v6 on v5

--- a/solution.py
+++ b/solution.py
@@ -65,7 +65,7 @@
     slots = lefts[0].shape[0]
     zero_slot = panel.shape[0] - 1
     col, layer = lax.axis_index("col"), lax.axis_index("depth")
-    width = 2 if pairs % 2 == 0 else 1
+    width = pairs
 
     def products(step, left, out):
         place = lax.rem(ring_place(col, cols) - step + cols, cols)

time: 21.7 us -> 21.7 us (level)
  no operation moved by 1% of the time
where the time goes in v6:
time: 21.7 us; the launch traced here: 21.5 us
  starting transfers between devices  10.7 us (49%)
  waiting for transfers between devices  6.62 us (31%)
  Pallas kernels  4.05 us (19%)
    ppermute x3, starting transfers between devices, turn(): lax.ppermute(block, axis, [(ring[i], ring[(i + step) % size]) for i in ra...  7.31 us
    ppermute x4, waiting for transfers between devices, exchange(): return lax.ppermute(block, axis, [(i, i ^ distance) for i in range(size)])  3.85 us
    ppermute x4, starting transfers between devices, exchange(): return lax.ppermute(block, axis, [(i, i ^ distance) for i in range(size)])  3.43 us
    ppermute x3, waiting for transfers between devices, turn(): lax.ppermute(block, axis, [(ring[i], ring[(i + step) % size]) for i in ra...  2.77 us
    pallas_call x3, Pallas kernels, add(): pl.pallas_call(functools.partial(add_kernel, steps, groups, share, bool(s...  2.26 us
    pallas_call x1, Pallas kernels, body(): pl.pallas_call(stage_kernel, out_shape=(pltpu.SMEM(pair_lists.shape, jnp....  0.95 us
    pallas_call x1, Pallas kernels, body(): pl.pallas_call(finish_kernel, out_shape=jax.ShapeDtypeStruct((share, widt...  0.72 us
  transfers between devices with their start and end apart: 7, of which 5 were waited for; matrix products, arithmetic and copies ran while one was open for 0% of the time, Pallas kernels for 14%

profile of v6, /device:TPU:0, one launch (start us, length us, event | category | flops | bytes accessed | tf_op | source)
XLA Modules:
  0.0 21.5 jit_solution(9313926398002435702)
XLA Ops:
  0.0 4.0 %collective-permute-start.2 = (bf16[4,128,128]{2,1,0:T(8,128)(2,1)}, bf16[4,128,128]{2,1,0:T(8,128)(2,1)S(1)}, u32[]{:S(2)}, u32[]{:S(2)}) collective-permute-start(bf16[4,128,128]{2,1,0:T(8,128)(2,1)} %bitcast.2), channel_id=1, source_target_pairs={{0,8},{8,12},{12,4},{4,0},{1,9},{9,13},{13,5},{5,1},{2,10},{10,14}... | collective-permute-start | bytes 393224 | tf_op jit(solution)/shard_map/ppermute | solution.py:34
  4.0 0.0 collective-permute-start.1
  4.0 1.5 %collective-permute-start = (bf16[4,128,128]{2,1,0:T(8,128)(2,1)}, bf16[4,128,128]{2,1,0:T(8,128)(2,1)S(1)}, u32[]{:S(2)}, u32[]{:S(2)}) collective-permute-start(bf16[4,128,128]{2,1,0:T(8,128)(2,1)} %bitcast.4), channel_id=1, source_target_pairs={{0,16},{16,0},{1,17},{17,1},{2,18},{18,2},{3,19},{19,3},{4,20},{20... | collective-permute-start | bytes 393224 | tf_op jit(solution)/shard_map/ppermute | solution.py:20
  5.6 1.0 %stage.1 = (s32[1,1,1,4,2,4,12]{6,5,4,3,2,1,0:T(4,128)S(4)}, bf16[4,128,128]{2,1,0:T(8,128)(2,1)S(1)}) custom-call(bf16[4,128,128]{2,1,0:T(8,128)(2,1)} %bitcast.5, s32[1,1,1,4,2,4,12]{6,5,4,3,2,1,0:T(4,128)} %lists.1), custom_call_target="tpu_custom_call" | custom-call | tf_op jit(solution)/shard_map/stage/pallas_call | solution.py:149
  6.5 1.7 %collective-permute-done.2.refs_1_ = bf16[4,128,128]{2,1,0:T(8,128)(2,1)S(1)} collective-permute-done((bf16[4,128,128]{2,1,0:T(8,128)(2,1)}, bf16[4,128,128]{2,1,0:T(8,128)(2,1)S(1)}, u32[]{:S(2)}, u32[]{:S(2)}) %collective-permute-start.2) | collective-permute-done | bytes 131104 | tf_op jit(solution)/shard_map/ppermute | solution.py:34
  8.3 3.3 %collective-permute-start.3 = (bf16[4,128,128]{2,1,0:T(8,128)(2,1)S(1)}, bf16[4,128,128]{2,1,0:T(8,128)(2,1)S(1)}, u32[]{:S(2)}, u32[]{:S(2)}) collective-permute-start(bf16[4,128,128]{2,1,0:T(8,128)(2,1)S(1)} %collective-permute-done.2.refs_1_), channel_id=1, source_target_pairs={{0,8},{8,12},{12,4},{4,0},{1,9},{9,13},{13,5},{5,1},{2,10},{10,14}... | collective-permute-start | bytes 393224 | tf_op jit(solution)/shard_map/ppermute | solution.py:34
  11.5 0.4 %collective-permute-done.1.refs_2_ = bf16[4,128,128]{2,1,0:T(8,128)(2,1)S(1)} collective-permute-done((bf16[4,128,128]{2,1,0:T(8,128)(2,1)}, bf16[4,128,128]{2,1,0:T(8,128)(2,1)S(1)}, u32[]{:S(2)}, u32[]{:S(2)}) %collective-permute-start.1) | collective-permute-done | bytes 131104 | tf_op jit(solution)/shard_map/ppermute | solution.py:34
  12.0 0.0 collective-permute-done.refs_1_
  12.0 1.4 %early_products.1 = (f32[3,128,128]{2,1,0:T(8,128)S(1)}, f32[3,128,128]{2,1,0:T(8,128)S(1)}, f32[3,128,128]{2,1,0:T(8,128)S(1)}, f32[3,128,128]{2,1,0:T(8,128)S(1)}) custom-call(s32[1,1,1,4,2,4,12]{6,5,4,3,2,1,0:T(4,128)S(4)} %get-tuple-element.14.lists, bf16[9,128,128]{2,1,0:T(8,128)(2,1)S(1)} %right_panel.1.panel, ...), custom_call_target="tpu_custom_call" | custom-call | flops 12079595520 | tf_op jit(solution)/shard_map/early_products/pallas_call | solution.py:187
  13.4 0.6 %collective-permute-done.3.refs_0_ = bf16[4,128,128]{2,1,0:T(8,128)(2,1)S(1)} collective-permute-done((bf16[4,128,128]{2,1,0:T(8,128)(2,1)S(1)}, bf16[4,128,128]{2,1,0:T(8,128)(2,1)S(1)}, u32[]{:S(2)}, u32[]{:S(2)}) %collective-permute-start.3) | collective-permute-done | bytes 131104 | tf_op jit(solution)/shard_map/ppermute | solution.py:34
  14.1 0.3 %late_products_first.1 = s16[400,128]{1,0:T(8,128)(2,1)S(1)} custom-call(s32[1,1,1,4,2,4,12]{6,5,4,3,2,1,0:T(4,128)S(4)} %get-tuple-element.14.lists, bf16[9,128,128]{2,1,0:T(8,128)(2,1)S(1)} %right_panel.1.panel, bf16[4,128,128]{2,1,0:T(8,128)(2,1)S(1)} %collective-permute-done.3.refs_0_, f32[3,128,128]{2,1,0:T(8,128)S(1)} %get-tuple-element.22.refs_1_), custom_call_target="tpu_custom_call" | custom-call | flops 1006632960 | tf_op jit(solution)/shard_map/late_products_first/pallas_call | solution.py:187
  14.4 0.1 collective-permute-start.5
  14.4 0.5 %late_products_rest.1 = (f32[3,128,128]{2,1,0:T(8,128)S(1)}, f32[3,128,128]{2,1,0:T(8,128)S(1)}, f32[3,128,128]{2,1,0:T(8,128)S(1)}) custom-call(s32[1,1,1,4,2,4,12]{6,5,4,3,2,1,0:T(4,128)S(4)} %get-tuple-element.14.lists, bf16[9,128,128]{2,1,0:T(8,128)(2,1)S(1)} %right_panel.1.panel, bf16[4,128,128]{2,1,0:T(8,128)(2,1)S(1)} %collective-permute-done.3.refs_0_, ...), custom_call_target="tpu_custom_call" | custom-call | flops 3019898880 | tf_op jit(solution)/shard_map/late_products_rest/pallas_call | solution.py:187
  15.0 0.5 %collective-permute-start.4 = (f32[3,128,128]{2,1,0:T(8,128)S(1)}, f32[3,128,128]{2,1,0:T(8,128)S(1)}, u32[]{:S(2)}, u32[]{:S(2)}) collective-permute-start(f32[3,128,128]{2,1,0:T(8,128)S(1)} %get-tuple-element.20), channel_id=1, source_target_pairs={{0,1},{1,0},{2,3},{3,2},{4,5},{5,4},{6,7},{7,6},{8,9},{9,8},{10,11... | collective-permute-start | bytes 589832 | tf_op jit(solution)/shard_map/ppermute | solution.py:20
  15.5 0.3 %collective-permute-done.5.came = s16[400,128]{1,0:T(8,128)(2,1)S(1)} collective-permute-done((s16[400,128]{1,0:T(8,128)(2,1)S(1)}, s16[400,128]{1,0:T(8,128)(2,1)S(1)}, u32[]{:S(2)}, u32[]{:S(2)}) %collective-permute-start.5) | collective-permute-done | bytes 102432 | tf_op jit(solution)/shard_map/ppermute | solution.py:20
  15.7 0.1 code.1
  15.8 1.3 %collective-permute-start.6 = (s16[400,128]{1,0:T(8,128)(2,1)S(1)}, s16[400,128]{1,0:T(8,128)(2,1)S(1)}, u32[]{:S(2)}, u32[]{:S(2)}) collective-permute-start(s16[400,128]{1,0:T(8,128)(2,1)S(1)} %code.1), channel_id=1, source_target_pairs={{0,3},{1,2},{2,1},{3,0},{4,7},{5,6},{6,5},{7,4},{8,11},{9,10},{10,... | collective-permute-start | bytes 307208 | tf_op jit(solution)/shard_map/ppermute | solution.py:20
  17.1 0.0 collective-permute-done.4.came
  17.2 3.6 %collective-permute-done.6.coded = s16[400,128]{1,0:T(8,128)(2,1)S(1)} collective-permute-done((s16[400,128]{1,0:T(8,128)(2,1)S(1)}, s16[400,128]{1,0:T(8,128)(2,1)S(1)}, u32[]{:S(2)}, u32[]{:S(2)}) %collective-permute-start.6) | collective-permute-done | bytes 102432 | tf_op jit(solution)/shard_map/ppermute | solution.py:20
  20.7 0.7 %finish.1 = f32[3,128,128]{2,1,0:T(8,128)} custom-call(f32[3,128,128]{2,1,0:T(8,128)S(1)} %get-tuple-element.19.kept, f32[3,128,128]{2,1,0:T(8,128)S(1)} %collective-permute-done.4.came, s16[400,128]{1,0:T(8,128)(2,1)S(1)} %collective-permute-done.6.coded), custom_call_target="tpu_custom_call" | custom-call | tf_op jit(solution)/shard_map/finish/pallas_call | solution.py:212
  (1 shorter events, 0.0 us)
Async XLA Ops:
  0.0 8.3 %collective-permute-start.2 = (bf16[4,128,128]{2,1,0:T(8,128)(2,1)}, bf16[4,128,128]{2,1,0:T(8,128)(2,1)S(1)}, u32[]{:S(2)}, u32[]{:S(2)}) collective-permute-start(bf16[4,128,128]{2,1,0:T(8,128)(2,1)} %bitcast.2), channel_id=1, source_target_pairs={{0,8},{8,12},{12,4},{4,0},{1,9},{9,13},{13,5},{5,1},{2,10},{10,14}... | collective-permute-start | bytes 393224 | tf_op jit(solution)/shard_map/ppermute | solution.py:34
  4.0 7.9 %collective-permute-start.1 = (bf16[4,128,128]{2,1,0:T(8,128)(2,1)}, bf16[4,128,128]{2,1,0:T(8,128)(2,1)S(1)}, u32[]{:S(2)}, u32[]{:S(2)}) collective-permute-start(bf16[4,128,128]{2,1,0:T(8,128)(2,1)} %bitcast.3), channel_id=1, source_target_pairs={{0,4},{8,0},{12,8},{4,12},{1,5},{9,1},{13,9},{5,13},{2,6},{10,2},{... | collective-permute-start | bytes 393224 | tf_op jit(solution)/shard_map/ppermute | solution.py:34
  4.0 7.9 %collective-permute-start = (bf16[4,128,128]{2,1,0:T(8,128)(2,1)}, bf16[4,128,128]{2,1,0:T(8,128)(2,1)S(1)}, u32[]{:S(2)}, u32[]{:S(2)}) collective-permute-start(bf16[4,128,128]{2,1,0:T(8,128)(2,1)} %bitcast.4), channel_id=1, source_target_pairs={{0,16},{16,0},{1,17},{17,1},{2,18},{18,2},{3,19},{19,3},{4,20},{20... | collective-permute-start | bytes 393224 | tf_op jit(solution)/shard_map/ppermute | solution.py:20
  8.3 5.8 %collective-permute-start.3 = (bf16[4,128,128]{2,1,0:T(8,128)(2,1)S(1)}, bf16[4,128,128]{2,1,0:T(8,128)(2,1)S(1)}, u32[]{:S(2)}, u32[]{:S(2)}) collective-permute-start(bf16[4,128,128]{2,1,0:T(8,128)(2,1)S(1)} %collective-permute-done.2.refs_1_), channel_id=1, source_target_pairs={{0,8},{8,12},{12,4},{4,0},{1,9},{9,13},{13,5},{5,1},{2,10},{10,14}... | collective-permute-start | bytes 393224 | tf_op jit(solution)/shard_map/ppermute | solution.py:34
  14.4 1.4 %collective-permute-start.5 = (s16[400,128]{1,0:T(8,128)(2,1)S(1)}, s16[400,128]{1,0:T(8,128)(2,1)S(1)}, u32[]{:S(2)}, u32[]{:S(2)}) collective-permute-start(s16[400,128]{1,0:T(8,128)(2,1)S(1)} %late_products_first.1), channel_id=1, source_target_pairs={{0,1},{1,0},{2,3},{3,2},{4,5},{5,4},{6,7},{7,6},{8,9},{9,8},{10,11... | collective-permute-start | bytes 307208 | tf_op jit(solution)/shard_map/ppermute | solution.py:20
  15.0 2.2 %collective-permute-start.4 = (f32[3,128,128]{2,1,0:T(8,128)S(1)}, f32[3,128,128]{2,1,0:T(8,128)S(1)}, u32[]{:S(2)}, u32[]{:S(2)}) collective-permute-start(f32[3,128,128]{2,1,0:T(8,128)S(1)} %get-tuple-element.20), channel_id=1, source_target_pairs={{0,1},{1,0},{2,3},{3,2},{4,5},{5,4},{6,7},{7,6},{8,9},{9,8},{10,11... | collective-permute-start | bytes 589832 | tf_op jit(solution)/shard_map/ppermute | solution.py:20
  15.8 4.9 %collective-permute-start.6 = (s16[400,128]{1,0:T(8,128)(2,1)S(1)}, s16[400,128]{1,0:T(8,128)(2,1)S(1)}, u32[]{:S(2)}, u32[]{:S(2)}) collective-permute-start(s16[400,128]{1,0:T(8,128)(2,1)S(1)} %code.1), channel_id=1, source_target_pairs={{0,3},{1,2},{2,1},{3,0},{4,7},{5,6},{6,5},{7,4},{8,11},{9,10},{10,... | collective-permute-start | bytes 307208 | tf_op jit(solution)/shard_map/ppermute | solution.py:20
